TPU v7x, 32 devices: a whole 2x2x4 slice. The times are simulated.
32 devices in a mesh: blk: 2 (over core), dp: 16 (over z, y, x).
Axes of the slice: x: 2, y: 2, z: 4, core: 2. Of those that a mesh axis runs over, the one named last changes fastest.
Arguments:
- inputs: bfloat16 [64, 1024, 768], P('dp', 'blk'), may hold values from -6 to 6
- cotangent: bfloat16 [64, 1024, 768], P('dp', 'blk'), may hold values from -6 to 6
- doc_lengths: int32 [64, 2], P('dp'), may hold values from 0 to 1024, as said below
- owner_list: int32 [12], replicated, may hold values from 0 to 15, as said below
- master: float32 [48, 768, 768], P('dp', 'blk'), as said below
- first_moment: float32 [48, 768, 768], P('dp', 'blk'), as said below
- second_moment: float32 [48, 768, 768], P('dp', 'blk'), as said below
- vectors: float32 [12, 768], replicated
- vector_first: float32 [12, 768], P(None, 'blk')
- vector_second: float32 [12, 768], P(None, 'blk'), as said below
Outputs:
- block_out: float32 [64, 1024, 768], P('dp', 'blk')
- input_grad: float32 [64, 1024, 768], P('dp', 'blk')
- new_master: float32 [48, 768, 768], P('dp', 'blk')
- new_first: float32 [48, 768, 768], P('dp', 'blk')
- new_second: float32 [48, 768, 768], P('dp', 'blk')
- new_vectors: float32 [12, 768], P(None, 'blk')
- new_vector_first: float32 [12, 768], P(None, 'blk')
- new_vector_second: float32 [12, 768], P(None, 'blk')
Inputs may be any that keep to these rules, and one draw needn't show every extreme that they name: `doc_lengths`: each row holds either one document (first entry 1024, second 0) or two of half of 1024 each; among the 4 rows of each aligned block both kinds occur. `owner_list`: one owner holds exactly 3 tiles and none holds more. `master`: slots that no tile names are not read. `first_moment`: slots that no tile names are not read. `second_moment`: entries are positive; slots that no tile names are not read. `vector_second`: entries are positive.
All inputs are finite; a program needn't handle non-finite values.
Results may differ from a plain program's by a relative error of at most 0.023.
Values may be sent and summed in bfloat16 or wider, within the bound.
A program may use at most 384 MiB of HBM per device.

v0:
```python
from functools import partial

import jax
import jax.numpy as jnp
from jax import lax
from jax.experimental import pallas as pl
from jax.experimental.pallas import tpu as pltpu
from jax.sharding import PartitionSpec as P

D = 768
FF = 3072
HEADS = 12
HEAD_DIM = 64
LEN = 1024
CAP = 3
STEP = 10
PIECES = 12


EPS_NORM = 1e-05
BETA_ONE = 0.9
BETA_TWO = 0.999
RATE = 0.04
VEC_RATE = 0.25
DECAY = 0.01
ADAM_EPS = 1e-08


def normalize(values_in, gain, shift):
    center = jnp.mean(values_in, axis=-1, keepdims=True)
    offset = values_in - center
    spread = jnp.mean(offset * offset, axis=-1, keepdims=True)
    return offset * lax.rsqrt(spread + EPS_NORM) * gain + shift


def adam_step(weight, grad, first, second, rate):
    first_new = BETA_ONE * first + (1.0 - BETA_ONE) * grad
    second_new = BETA_TWO * second + (1.0 - BETA_TWO) * grad * grad
    corrected = (
        first_new
        / (1.0 - BETA_ONE**STEP)
        / (jnp.sqrt(second_new / (1.0 - BETA_TWO**STEP)) + ADAM_EPS)
    )
    return (weight - rate * (corrected + DECAY * weight), first_new, second_new)


def shards_any(
    inputs,
    cotangent,
    doc_lengths,
    owner_list,
    master,
    first_moment,
    second_moment,
    vectors,
    vector_first,
    vector_second,
):
    rows_here, span, width = inputs.shape
    tokens_here = rows_here * span
    fold = FF // D
    scale = HEAD_DIM ** (-0.5)
    place = lax.axis_index("blk")
    f32 = jnp.float32
    b16 = jnp.bfloat16
    order = jnp.arange(PIECES)
    same_owner = owner_list[:, None] == owner_list[None, :]
    ranks = jnp.sum(same_owner & (order[None, :] < order[:, None]), axis=1)
    slot_of = owner_list * CAP + ranks

    mine = (owner_list == lax.axis_index("dp"))[:, None, None]
    tile_rows = lax.psum(jnp.where(mine, master[ranks], 0.0).astype(b16), "dp")
    tiles = lax.all_gather(tile_rows, "blk", axis=1, tiled=True)
    query_weight = tiles[0]
    key_weight = tiles[1]
    value_weight = tiles[2]
    out_weight = tiles[3]
    up_weight = jnp.transpose(tiles[4 : 4 + fold], (1, 0, 2)).reshape(width, FF)
    down_weight = tiles[4 + fold :].reshape(FF, width)
    flat_in = inputs.reshape(tokens_here, width).astype(f32)
    normed_one = normalize(flat_in, vectors[0], vectors[1]).astype(b16)
    queries = (jnp.dot(normed_one, query_weight, preferred_element_type=f32) + vectors[4]).astype(
        b16
    )
    keys_here = jnp.dot(normed_one, key_weight, preferred_element_type=f32).astype(b16)
    values_here = (
        jnp.dot(normed_one, value_weight, preferred_element_type=f32) + vectors[5]
    ).astype(b16)
    query_heads = queries.reshape(rows_here, span, HEADS, HEAD_DIM)
    first_len = doc_lengths[:, 0]
    query_seg = (place * span + jnp.arange(span))[None, :] >= first_len[:, None]

    def block_scores(key_block, start):
        count = key_block.shape[1]
        key_heads = key_block.reshape(rows_here, count, HEADS, HEAD_DIM)
        raw = (
            jnp.einsum("rqhd,rkhd->rhqk", query_heads, key_heads, preferred_element_type=f32)
            * scale
        )
        key_seg = (start + jnp.arange(count))[None, :] >= first_len[:, None]
        allowed = query_seg[:, None, :, None] == key_seg[:, None, None, :]
        return (raw, allowed)

    key_rows = keys_here.reshape(rows_here, span, width)
    value_rows = values_here.reshape(rows_here, span, width)
    top = jnp.full((rows_here, HEADS, span), -1e30, f32)
    key_block = lax.all_gather(key_rows, "blk", axis=1, tiled=True)
    value_block = lax.all_gather(value_rows, "blk", axis=1, tiled=True)
    count = key_block.shape[1]
    raw, allowed = block_scores(key_block, jnp.int32(0))
    new_top = jnp.maximum(top, jnp.max(jnp.where(allowed, raw, -1e30), axis=-1))
    weights = jnp.where(allowed, jnp.exp(raw - new_top[..., None]), 0.0)
    value_heads = value_block.reshape(rows_here, count, HEADS, HEAD_DIM)
    update = jnp.einsum(
        "rhqk,rkhd->rhqd", weights.astype(b16), value_heads, preferred_element_type=f32
    )
    total = jnp.sum(weights, axis=-1)
    log_total = new_top + jnp.log(total)
    context_raw = update / total[..., None]
    context_low = jnp.transpose(context_raw, (0, 2, 1, 3)).reshape(tokens_here, width).astype(b16)
    residual = flat_in + (jnp.dot(context_low, out_weight, preferred_element_type=f32) + vectors[6])
    normed_two = normalize(residual, vectors[2], vectors[3]).astype(b16)
    hidden = jnp.dot(normed_two, up_weight, preferred_element_type=f32) + vectors[8:].reshape(FF)
    gelu_exact = partial(jax.nn.gelu, approximate=False)
    active, gelu_pull = jax.vjp(gelu_exact, hidden)
    active_low = active.astype(b16)
    block_out = (
        residual + (jnp.dot(active_low, down_weight, preferred_element_type=f32) + vectors[7])
    ).reshape(rows_here, span, width)
    grad_out = cotangent.reshape(tokens_here, width)
    down_grad = jnp.einsum("tf,td->fd", active_low, grad_out, preferred_element_type=f32)
    down_sum = jnp.sum(grad_out, axis=0, dtype=f32)
    grad_active = jnp.einsum("td,fd->tf", grad_out, down_weight, preferred_element_type=f32)
    grad_hidden = gelu_pull(grad_active)[0].astype(b16)
    up_grad = jnp.einsum("td,tf->df", normed_two, grad_hidden, preferred_element_type=f32)
    up_sum = jnp.sum(grad_hidden, axis=0, dtype=f32)
    ffn_tiles = jnp.concatenate(
        [
            jnp.transpose(up_grad.reshape(width, fold, width), (1, 0, 2)),
            down_grad.reshape(fold, width, width),
        ],
        axis=0,
    )
    grad_normed_two = jnp.einsum("tf,df->td", grad_hidden, up_weight, preferred_element_type=f32)
    unused, second_pull = jax.vjp(normalize, residual, vectors[2], vectors[3])
    residual_part, gain_two_grad, shift_two_grad = second_pull(grad_normed_two)
    grad_residual = grad_out.astype(f32) + residual_part
    grad_attended = grad_residual.astype(b16)
    out_grad = jnp.einsum("tm,td->md", context_low, grad_attended, preferred_element_type=f32)
    out_sum = jnp.sum(grad_attended, axis=0, dtype=f32)
    grad_context = jnp.einsum(
        "td,md->tm", grad_attended, out_weight, preferred_element_type=f32
    ).astype(b16)
    grad_heads = grad_context.reshape(rows_here, span, HEADS, HEAD_DIM)
    delta = jnp.einsum("rqhd,rhqd->rhq", grad_heads.astype(f32), context_raw)
    key_all, value_all = (
        lax.all_gather(key_rows, "blk", axis=1, tiled=True),
        lax.all_gather(value_rows, "blk", axis=1, tiled=True),
    )
    key_size = min(512, LEN)

    def back_block(index, carry):
        grad_query, key_total, value_total = carry
        start = index * key_size
        key_block = lax.dynamic_slice_in_dim(key_all, start, key_size, 1)
        value_block = lax.dynamic_slice_in_dim(value_all, start, key_size, 1)
        raw, allowed = block_scores(key_block, start)
        weights_back = jnp.where(allowed, jnp.exp(raw - log_total[..., None]), 0.0)
        key_heads = key_block.reshape(rows_here, key_size, HEADS, HEAD_DIM)
        value_heads = value_block.reshape(rows_here, key_size, HEADS, HEAD_DIM)
        value_grad = jnp.einsum(
            "rhqk,rqhd->rkhd", weights_back.astype(b16), grad_heads, preferred_element_type=f32
        )
        weight_grad = jnp.einsum(
            "rqhd,rkhd->rhqk", grad_heads, value_heads, preferred_element_type=f32
        )
        score_grad = (weights_back * (weight_grad - delta[..., None])).astype(b16)
        grad_query = (
            grad_query
            + jnp.einsum("rhqk,rkhd->rqhd", score_grad, key_heads, preferred_element_type=f32)
            * scale
        )
        key_grad = (
            jnp.einsum("rhqk,rqhd->rkhd", score_grad, query_heads, preferred_element_type=f32)
            * scale
        )
        key_total = lax.dynamic_update_slice_in_dim(
            key_total, key_grad.reshape(rows_here, key_size, width), start, 1
        )
        value_total = lax.dynamic_update_slice_in_dim(
            value_total, value_grad.reshape(rows_here, key_size, width), start, 1
        )
        return (grad_query, key_total, value_total)

    zero_rows = jnp.zeros((rows_here, LEN, width), f32)
    grad_query, key_total, value_total = lax.fori_loop(
        0,
        LEN // key_size,
        back_block,
        (jnp.zeros((rows_here, span, HEADS, HEAD_DIM), f32), zero_rows, zero_rows),
    )
    key_grad_here, value_grad_here = (
        lax.psum_scatter(
            key_total.astype(jnp.bfloat16), "blk", scatter_dimension=1, tiled=True
        ).astype(jnp.float32),
        lax.psum_scatter(
            value_total.astype(jnp.bfloat16), "blk", scatter_dimension=1, tiled=True
        ).astype(jnp.float32),
    )
    query_low = grad_query.reshape(tokens_here, width).astype(b16)
    key_low = key_grad_here.reshape(tokens_here, width).astype(b16)
    value_low = value_grad_here.reshape(tokens_here, width).astype(b16)
    query_tile = jnp.einsum("td,te->de", normed_one, query_low, preferred_element_type=f32)
    key_tile = jnp.einsum("td,te->de", normed_one, key_low, preferred_element_type=f32)
    value_tile = jnp.einsum("td,te->de", normed_one, value_low, preferred_element_type=f32)
    grad_normed_one = (
        jnp.einsum("te,de->td", query_low, query_weight, preferred_element_type=f32)
        + jnp.einsum("te,de->td", key_low, key_weight, preferred_element_type=f32)
        + jnp.einsum("te,de->td", value_low, value_weight, preferred_element_type=f32)
    )
    unused, first_pull = jax.vjp(normalize, flat_in, vectors[0], vectors[1])
    input_part, gain_one_grad, shift_one_grad = first_pull(grad_normed_one)
    input_grad = (grad_residual + input_part).reshape(rows_here, span, width)
    vector_grads = jnp.concatenate(
        [
            jnp.stack(
                [
                    gain_one_grad,
                    shift_one_grad,
                    gain_two_grad,
                    shift_two_grad,
                    jnp.sum(query_low, axis=0, dtype=f32),
                    jnp.sum(value_low, axis=0, dtype=f32),
                    out_sum,
                    down_sum,
                ]
            ),
            up_sum.reshape(fold, width),
        ],
        axis=0,
    )
    attn_tiles = jnp.stack([query_tile, key_tile, value_tile, out_grad])
    piece_share, vector_share = (
        lax.psum_scatter(
            jnp.concatenate([attn_tiles, ffn_tiles], axis=0).astype(jnp.bfloat16),
            "blk",
            scatter_dimension=1,
            tiled=True,
        ).astype(jnp.float32),
        lax.psum_scatter(
            vector_grads.astype(jnp.bfloat16), "blk", scatter_dimension=1, tiled=True
        ).astype(jnp.float32),
    )
    own_slots = lax.axis_index("dp") * CAP + jnp.arange(CAP)
    pick = (own_slots[:, None] == slot_of[None, :]).astype(f32)
    occupied = jnp.sum(pick, axis=1)[:, None, None]
    total_share, vector_total = (
        lax.psum(piece_share.astype(jnp.bfloat16), "dp").astype(jnp.float32),
        lax.psum(vector_share.astype(jnp.bfloat16), "dp").astype(jnp.float32),
    )
    slot_grads = jnp.einsum("cp,prd->crd", pick, total_share, precision=lax.Precision.HIGHEST)
    new_master, new_first, new_second = adam_step(
        master, slot_grads, first_moment, second_moment, RATE
    )
    columns = vector_first.shape[1]
    vector_cols = lax.dynamic_slice_in_dim(vectors, place * columns, columns, 1)
    new_vectors, new_vector_first, new_vector_second = adam_step(
        vector_cols, vector_total, vector_first, vector_second, VEC_RATE
    )
    return (
        block_out,
        input_grad,
        new_master * occupied,
        new_first * occupied,
        new_second * occupied,
        new_vectors,
        new_vector_first,
        new_vector_second,
    )


f32 = jnp.float32
b16 = jnp.bfloat16
LOG2E = 1.4426950408889634
MIB = 1024 * 1024
PAIRS = HEADS // 2
PAIR = 2 * HEAD_DIM


def dot_nn(left, right):
    return lax.dot_general(left, right, (((1,), (0,)), ((), ())), preferred_element_type=f32)


def dot_nt(left, right):
    return lax.dot_general(left, right, (((1,), (1,)), ((), ())), preferred_element_type=f32)


def dot_tn(left, right):
    return lax.dot_general(left, right, (((0,), (0,)), ((), ())), preferred_element_type=f32)


def norm_parts(values_in):
    center = jnp.mean(values_in, axis=-1, keepdims=True)
    offset = values_in - center
    spread = jnp.mean(offset * offset, axis=-1, keepdims=True)
    rstd = lax.rsqrt(spread + EPS_NORM)
    return offset * rstd, rstd


def norm_back(grad, unit, rstd, gain):
    scaled = grad * gain
    first = jnp.mean(scaled, axis=-1, keepdims=True)
    second = jnp.mean(scaled * unit, axis=-1, keepdims=True)
    return rstd * (scaled - first - unit * second)


def gelu_parts(value):
    bell = jnp.exp2(value * value * (-0.5 * LOG2E))
    ratio = pl.reciprocal(1.0 + (0.3275911 * 0.7071067811865476) * jnp.abs(value))
    poly = 0.5 * 1.061405429
    poly = poly * ratio + 0.5 * -1.453152027
    poly = poly * ratio + 0.5 * 1.421413741
    poly = poly * ratio + 0.5 * -0.284496736
    poly = poly * ratio + 0.5 * 0.254829592
    tail = poly * ratio * bell
    cdf = jnp.where(value >= 0.0, 1.0 - tail, tail)
    return value * cdf, cdf + value * (bell * 0.3989422804014327)


def head_only(block, head):
    lane = lax.broadcasted_iota(jnp.int32, block.shape, 1)
    keep = (lane >= head * HEAD_DIM) & (lane < (head + 1) * HEAD_DIM)
    return jnp.where(keep, block, jnp.zeros_like(block))


def feed_kernel(
    c_ref, o_ref, x_ref, g_ref, w_ref, vec_ref,
    y_ref, r_ref, d_ref, sums_ref, tiles_ref,
    acc_ref, stage_ref, sem_ref,
):
    fold = FF // D
    step = pl.program_id(0)

    @pl.when(step == 0)
    def clear():
        acc_ref[...] = jnp.zeros_like(acc_ref)
        sums_ref[...] = jnp.zeros_like(sums_ref)

    residual = x_ref[...].astype(f32) + (dot_nn(c_ref[...], w_ref[0]) + vec_ref[6:7, :])
    unit, rstd = norm_parts(residual)
    gain = vec_ref[2:3, :]
    normed = (unit * gain + vec_ref[3:4, :]).astype(b16)
    turned = normed.T
    cot = g_ref[...]
    out = residual + vec_ref[7:8, :]
    grad = jnp.zeros_like(out)

    for part in range(fold):
        hidden = dot_nn(normed, w_ref[1 + part]) + vec_ref[8 + part : 9 + part, :]
        pulled = dot_nt(cot, w_ref[1 + fold + part])
        active, slope = gelu_parts(hidden)
        active = active.astype(b16)
        pulled = (pulled * slope).astype(b16)
        out = out + dot_nn(active, w_ref[1 + fold + part])
        grad = grad + dot_nt(pulled, w_ref[1 + part])
        acc_ref[1 + part] += dot_nn(turned, pulled)
        acc_ref[1 + fold + part] += dot_tn(active, cot)
        sums_ref[8 + part : 9 + part, :] += jnp.sum(pulled.astype(f32), 0, keepdims=True)
    y_ref[...] = out.astype(b16)
    wide = cot.astype(f32)
    sums_ref[2:3, :] += jnp.sum(grad * unit, 0, keepdims=True)
    sums_ref[3:4, :] += jnp.sum(grad, 0, keepdims=True)
    sums_ref[7:8, :] += jnp.sum(wide, 0, keepdims=True)
    back = wide + norm_back(grad, unit, rstd, gain)
    r_ref[...] = back.astype(b16)
    low = back.astype(b16)
    sums_ref[6:7, :] += jnp.sum(low.astype(f32), 0, keepdims=True)
    d_ref[...] = dot_nt(w_ref[0], low).astype(b16)
    acc_ref[0] += dot_nn(o_ref[...], low)

    @pl.when(step == pl.num_programs(0) - 1)
    def send():
        count = 1 + 2 * fold
        copies = []
        for part in range(count):
            if part >= 2:
                copies[part - 2].wait()
            stage_ref[part % 2] = acc_ref[part].astype(b16)
            copy = pltpu.make_async_copy(stage_ref.at[part % 2], tiles_ref.at[part], sem_ref.at[part % 2])
            copy.start()
            copies.append(copy)
        copies[count - 2].wait()
        copies[count - 1].wait()


def feed(context, turned, x, cot, weights, vectors):
    tokens = x.shape[0]
    size = 256
    count = 1 + 2 * (FF // D)
    token_block = pl.BlockSpec((size, D), lambda i: (i, 0))
    turned_block = pl.BlockSpec((D, size), lambda i: (0, i))
    return pl.pallas_call(
        feed_kernel,
        grid=(tokens // size,),
        in_specs=[
            token_block,
            turned_block,
            token_block,
            token_block,
            pl.BlockSpec((count, D, D), lambda i: (0, 0, 0), pipeline_mode=pl.Buffered(1)),
            pl.BlockSpec((PIECES, D), lambda i: (0, 0)),
        ],
        out_specs=[
            token_block,
            token_block,
            turned_block,
            pl.BlockSpec((16, D), lambda i: (0, 0)),
            pl.BlockSpec(memory_space=pl.ANY),
        ],
        out_shape=[
            jax.ShapeDtypeStruct((tokens, D), b16),
            jax.ShapeDtypeStruct((tokens, D), b16),
            jax.ShapeDtypeStruct((D, tokens), b16),
            jax.ShapeDtypeStruct((16, D), f32),
            jax.ShapeDtypeStruct((count, D, D), b16),
        ],
        scratch_shapes=[
            pltpu.VMEM((count, D, D), f32),
            pltpu.VMEM((2, D, D), b16),
            pltpu.SemaphoreType.DMA((2,)),
        ],
        compiler_params=pltpu.CompilerParams(vmem_limit_bytes=60 * MIB),
        cost_estimate=pl.CostEstimate(
            flops=6 * count * tokens * D * D,
            bytes_accessed=18 * tokens * D + 4 * count * D * D,
            transcendentals=2 * tokens * FF,
        ),
        name="feed",
    )(context, turned, x, cot, weights, vectors)


MESH = pl.DeviceIdType.MESH
HALF = D // 2
FLOWS = 2
FLOW = HALF // FLOWS
NEAR = FLOW // 2
KEEP = NEAR // 2
WIDE = 3 * PAIR
REST = PIECES - 3
GROUPS = ((0, 1), (1, 2), (3, 3))
CHUNKS = len(GROUPS)


class Place:
    def __init__(self):
        self.me = lax.axis_index("dp")
        self.core = lax.axis_index("blk")
        self.bits = [lax.rem(self.me // weight, 2) for weight in (1, 2, 4, 8)]
        self.chips = [
            self.me + weight - 2 * weight * bit for weight, bit in zip((1, 2, 4, 8), self.bits)
        ]
        self.partners = [{"dp": chip} for chip in self.chips]
        low, high = self.bits[2:]
        self.inner = low != high
        self.across = {"dp": self.me + 4 - 8 * low + 8 - 16 * high}
        self.other = 1 - self.core
        self.twin = {"blk": self.other}

    def greet(self):
        barrier = pltpu.get_barrier_semaphore()
        for device in self.partners + [self.across, self.twin]:
            pl.semaphore_signal(barrier, 1, device_id=device, device_id_type=MESH)
        pl.semaphore_wait(barrier, 6)

    def flow(self, index):
        first, second = (0, 1) if index == 0 else (1, 0)
        base = index * FLOW
        near = base + self.bits[first] * NEAR
        far = base + NEAR - self.bits[first] * NEAR
        keep = near + self.bits[second] * KEEP
        give = near + KEEP - self.bits[second] * KEEP
        return first, second, near, far, keep, give


def remote(source, target, send, receive, device):
    return pltpu.make_async_remote_copy(
        src_ref=source,
        dst_ref=target,
        send_sem=send,
        recv_sem=receive,
        device_id=device,
        device_id_type=MESH,
    )


def rows_at(start, count):
    return pl.ds(pl.multiple_of(start, 16), count)


class Spread:
    def __init__(self, place, owner, rank, slots, land, gift, sems):
        self.place, self.owner, self.rank = place, owner, rank
        self.slots, self.land, self.gift, self.sems = slots, land, gift, sems

    def cols(self, chunk):
        return pl.ds(GROUPS[chunk][0] * PAIR, GROUPS[chunk][1] * PAIR)

    def first_copy(self, chunk, index):
        first, second, near, far, keep, give = self.place.flow(index)
        return remote(
            self.slots.at[:, rows_at(far, NEAR), self.cols(chunk)],
            self.land[chunk].at[index],
            self.sems[0].at[chunk, index, 0],
            self.sems[1].at[chunk, index, 0],
            self.place.partners[first],
        )

    def second_copy(self, chunk, index, which):
        first, second, near, far, keep, give = self.place.flow(index)
        if which == 0:
            source = self.slots.at[:, rows_at(give, KEEP), self.cols(chunk)]
        else:
            source = self.land[chunk].at[index, :, rows_at(give - near, KEEP)]
        return remote(
            source,
            self.gift[chunk].at[index, pl.ds(which * CAP, CAP)],
            self.sems[0].at[chunk, index, 1 + which],
            self.sems[1].at[chunk, index, 1 + which],
            self.place.partners[second],
        )

    def step(self, chunk, index):
        for flow in range(FLOWS):
            if index == 0:
                self.first_copy(chunk, flow).start()
                self.second_copy(chunk, flow, 0).start()
            if index == 1:
                self.first_copy(chunk, flow).wait()
                self.second_copy(chunk, flow, 1).start()
            if index == 2:
                self.second_copy(chunk, flow, 0).wait()
                self.second_copy(chunk, flow, 1).wait()

    def piece(self, tile, index, chunk, start, count):
        first, second, near, far, keep, give = self.place.flow(index)
        owner, rank = self.owner[tile], self.rank[tile]
        bits = [lax.rem(owner, 2), lax.rem(owner // 2, 2)]
        apart = [bit != mine for bit, mine in zip(bits, self.place.bits)]
        cols = pl.ds(start, count)
        mine = self.slots[rank, rows_at(keep, KEEP), pl.ds(GROUPS[chunk][0] * PAIR + start, count)]
        firsts = self.land[chunk][index, rank, rows_at(keep - near, KEEP), cols]
        gifts = self.gift[chunk][index, jnp.where(apart[first], CAP, 0) + rank, :, cols]
        value = jnp.where(apart[second], gifts, jnp.where(apart[first], firsts, mine))
        layer = owner // 4 == self.place.me // 4
        return jnp.where(layer, value, jnp.zeros_like(value))


class Column:
    steps = 4

    def __init__(self, place, kept, land, sems):
        self.place, self.kept, self.land, self.sems = place, kept, land, sems

    def copy(self, index):
        device = self.place.across if index == 1 else self.place.partners[2]
        return remote(
            self.kept, self.land.at[index % 2], self.sems[0].at[index], self.sems[1].at[index], device
        )

    def add(self, index):
        self.kept[...] = (self.kept[...].astype(f32) + self.land[index].astype(f32)).astype(b16)


def both_flows(flow):
    return pl.ds(flow * KEEP, KEEP)


def column_step(place, column, index):
    @pl.when(place.inner)
    def inner():
        if index == 1:
            column.copy(0).wait_recv()
            column.add(0)
            column.copy(1).start()
        if index == 2:
            column.copy(1).wait()
            column.add(1)
            column.copy(2).start()
        if index == 3:
            column.copy(2).wait_send()

    @pl.when(jnp.logical_not(place.inner))
    def outer():
        if index == 0:
            column.copy(0).start()
        if index == 1:
            column.copy(0).wait_send()
        if index == 3:
            column.copy(2).wait_recv()
            column.kept[...] = column.land[0]


class Item:
    steps = 7

    def __init__(self, place, work, kept, land, sems, load, store=None):
        self.place, self.work, self.kept, self.land, self.sems = place, work, kept, land, sems
        self.load, self.store = load, store
        self.base = place.core * HALF

    def copy(self, flow, index):
        first, second, near, far, keep, give = self.place.flow(flow)
        kept = self.work.at[:, rows_at(self.base + keep, KEEP)]
        half = self.work.at[:, rows_at(self.base + near, NEAR)]
        source, device = [
            (kept, self.place.partners[second]),
            (half, self.place.partners[first]),
        ][index]
        number = 3 + 2 * flow + index
        return remote(source, source, self.sems[0].at[number], self.sems[1].at[number], device)

    def pair(self):
        rows = self.work.at[:, rows_at(self.base, HALF)]
        return remote(rows, rows, self.sems[0].at[7], self.sems[1].at[7], self.place.twin)

    def step(self, index):
        if index == 0:
            for flow in range(FLOWS):
                self.load(self.kept, both_flows(flow), flow)
        if index <= 3:
            column_step(self.place, Column(self.place, self.kept, self.land, self.sems), index)
        for flow in range(FLOWS):
            if index == 3:
                rows = rows_at(self.base + self.place.flow(flow)[4], KEEP)
                self.work[:, rows] = self.kept[:, both_flows(flow)]
            if 4 <= index <= 5:
                self.copy(flow, index - 4).wait()
            if 3 <= index <= 4:
                self.copy(flow, index - 3).start()
        if index == 5:
            self.pair().start()
        if index == 6:
            self.pair().wait()
            self.store().start()


REST_GROUPS = tuple((index, 1) for index in range(REST))
PAIR_CHUNK = (0, 1, 1, 2, 2, 2)
FRONT_PAIRS = (2, 4, 5, 6, 7, 8)
FRONT_REST = (6, 7, 8, 9, 10, 11, 12, 13, 14)
FRONT_LEAD = 9


def front_kernel(
    owner, lengths, master, vec_ref, x_in, c_in,
    x_out, c_out, n_out, one_out, two_out, q_ref, k_ref, v_ref, p_ref, r_ref, o_ref, ctx_ref,
    rank, rows_ref, normed, keys, turned_values, scores, slots,
    land_one, land_two, land_three, gift_one, gift_two, gift_three,
    one, one_kept, one_land, two, two_kept, two_land,
    spread_send, spread_recv, one_send, one_recv, two_send, two_recv,
    swap_send, swap_recv, swap_local, store_sem,
):
    pair = pl.program_id(0)
    row = pl.program_id(1)
    grid_step = pair * 2 + row
    place = Place()
    rows, span = x_in.shape[0] // 2, x_in.shape[1]
    land = (land_one, land_two, land_three)
    gift = (gift_one, gift_two, gift_three)
    spread = Spread(place, owner, rank, slots, land, gift, (spread_send, spread_recv))

    def swaps(index):
        source, target = [(x_in, rows_ref), (c_in, c_out)][index]
        here = pl.ds(place.core * span, span)
        near = pltpu.make_async_copy(
            source.at[pl.ds(place.core * rows, rows)], target.at[:, here], swap_local.at[index]
        )
        far = remote(
            source.at[pl.ds(place.other * rows, rows)],
            target.at[:, here],
            swap_send.at[index],
            swap_recv.at[index],
            place.twin,
        )
        return near, far

    def row_store():
        return pltpu.make_async_copy(rows_ref, x_out, store_sem.at[PAIRS + REST])

    def normed_store():
        return pltpu.make_async_copy(normed, n_out, store_sem.at[PAIRS + REST + 1])

    def pair_item(group):
        span_of = pl.ds(group, 1)

        def load(work, where, flow):
            chunk = PAIR_CHUNK[group]
            for tile in range(3):
                part = spread.piece(tile, flow, chunk, (group - GROUPS[chunk][0]) * PAIR, PAIR)
                work[0, where, pl.ds(tile * PAIR, PAIR)] = part

        def store():
            return pltpu.make_async_copy(one.at[span_of], one_out.at[span_of], store_sem.at[group])

        sems = (one_send.at[group], one_recv.at[group])
        return Item(place, one.at[span_of], one_kept.at[span_of], one_land.at[:, span_of], sems, load, store)

    def rest_item(group):
        first, count = REST_GROUPS[group]
        span_of = pl.ds(first, count)

        def load(work, where, flow):
            for index in range(count):
                for chunk, (start, wide) in enumerate(GROUPS):
                    part = spread.piece(3 + first + index, flow, chunk, 0, wide * PAIR)
                    work[index, where, pl.ds(start * PAIR, wide * PAIR)] = part

        def store():
            return pltpu.make_async_copy(
                two.at[span_of], two_out.at[span_of], store_sem.at[PAIRS + group]
            )

        sems = (two_send.at[group], two_recv.at[group])
        return Item(place, two.at[span_of], two_kept.at[span_of], two_land.at[:, span_of], sems, load, store)

    def tick(number, odd):
        for chunk in range(CHUNKS):
            if odd == 0 and 0 <= number - 2 * chunk <= 2:
                spread.step(chunk, number - 2 * chunk)
        starts = [(pair_item, group, start) for group, start in enumerate(FRONT_PAIRS)]
        starts += [(rest_item, group, start) for group, start in enumerate(FRONT_REST)]
        for make, group, start in starts:
            if group % 2 == odd and 0 <= number - start < Item.steps:
                make(group).step(number - start)

    def both(number):
        tick(number, 0)
        tick(number, 1)

    @pl.when(grid_step == 0)
    def lead():
        slots[...] = master[...].astype(b16)
        for tile in range(PIECES):
            count = jnp.int32(0)
            for before in range(tile):
                count = count + (owner[before] == owner[tile]).astype(jnp.int32)
            rank[tile] = jnp.minimum(count, CAP - 1)
        place.greet()
        for copy in swaps(0):
            copy.start()
        both(0)
        for copy in swaps(1):
            copy.start()
        for copy in swaps(0):
            copy.wait()
        row_store().start()

        def norm_rows(index, carry):
            for part in range(rows):
                for block in range(4):
                    where = pl.ds(pl.multiple_of(index * 128 + block * 32, 32), 32)
                    unit, unused = norm_parts(rows_ref[part, where].astype(f32))
                    low = (unit * vec_ref[0:1, :] + vec_ref[1:2, :]).astype(b16)
                    normed[pl.ds(pl.multiple_of(part * LEN + index * 128 + block * 32, 32), 32)] = low
            return carry

        both(1)
        lax.fori_loop(0, LEN // 128, norm_rows, 0)
        normed_store().start()
        for number in range(2, FRONT_LEAD):
            both(number)

    for number in range(2 * PAIRS):
        pl.when(grid_step == number)(partial(tick, FRONT_LEAD + number, 0))

    @pl.when(row == 0)
    def project():
        lanes = pl.ds(pl.multiple_of(pair * PAIR, PAIR), PAIR)
        weight = one[pair]

        def part(index, carry):
            where = pl.ds(pl.multiple_of(index * 512, 512), 512)
            both = dot_nn(normed[where], weight)
            queries = both[:, :PAIR] + vec_ref[4:5, lanes]
            queries = (queries * (HEAD_DIM**-0.5 * LOG2E)).astype(b16)
            q_ref[:, where] = queries.T
            low = both[:, PAIR : 2 * PAIR].astype(b16)
            keys[where] = low
            k_ref[:, where] = low.T
            values = (both[:, 2 * PAIR :] + vec_ref[5:6, lanes]).astype(b16)
            v_ref[where] = values
            turned_values[:, where] = values.T
            return carry

        lax.fori_loop(0, normed.shape[0] // 512, part, 0)

    half = LEN // 2
    start = pl.multiple_of(row * LEN, LEN)
    split = lengths[place.core * rows + row, 0] < LEN
    shift = jnp.where(split, jnp.float32(-1e30), jnp.float32(0.0))

    quarter = LEN // 4
    units = [(head, step) for head in range(2) for step in range(2)]

    def score_block(unit, block, peak):
        head, step = units[unit]
        rows_here = pl.ds(pl.multiple_of(start + block * quarter, quarter), quarter)
        queries = q_ref[:, pl.ds(pl.multiple_of(start + step * half, half), half)]
        raw = dot_nn(head_only(keys[rows_here], head), queries)
        if block // 2 != step:
            raw = raw + shift
        scores[unit % 2, block * quarter : (block + 1) * quarter] = raw
        best = jnp.max(raw.reshape(-1, 8, half), axis=0)
        return best if peak is None else jnp.maximum(peak, best)

    def context_block(unit, block, total):
        head, step = units[unit]
        part = slice(head * HEAD_DIM, (head + 1) * HEAD_DIM)
        cols = pl.ds(pl.multiple_of(start + block * quarter, quarter), quarter)
        here = slice(step * half, (step + 1) * half)
        term = dot_nn(
            turned_values[part, cols], p_ref[head, block * quarter : (block + 1) * quarter, here]
        )
        return term if total is None else total + term

    def context_store(unit, total, recip):
        head, step = units[unit]
        part = slice(head * HEAD_DIM, (head + 1) * HEAD_DIM)
        o_ref[part, step * half : (step + 1) * half] = (total * recip).astype(b16)

    peak = None
    for block in range(4):
        peak = score_block(0, block, peak)
    before = None
    for unit, (head, step) in enumerate(units):
        if unit == 2:
            for number in range(2 * PAIRS):
                pl.when(grid_step == number)(partial(tick, FRONT_LEAD + number, 1))
        here = slice(step * half, (step + 1) * half)
        top = jnp.max(peak, 0, keepdims=True)
        total = jnp.zeros((8, half), f32)
        peak, context = None, None
        for block in range(4):
            if unit + 1 < len(units):
                peak = score_block(unit + 1, block, peak)
            for small in range(4 * block, 4 * block + 4):
                rows_here = slice(small * 64, (small + 1) * 64)
                value = jnp.exp2(scores[unit % 2, rows_here] - top)
                total = total + jnp.sum(value.reshape(-1, 8, half), axis=0)
                p_ref[head, rows_here, here] = value.astype(b16)
            if unit > 0:
                context = context_block(unit - 1, block, context)
        if unit > 0:
            context_store(unit - 1, context, before)
        before = 1.0 / jnp.sum(total, 0, keepdims=True)
        r_ref[0, head : head + 1, here] = before
    context = None
    for block in range(4):
        context = context_block(3, block, context)
    context_store(3, context, before)
    ctx_ref[...] = o_ref[...].T

    @pl.when(grid_step == 2 * PAIRS - 1)
    def finish_copies():
        for copy in swaps(1):
            copy.wait()
        row_store().wait()
        normed_store().wait()
        for group in range(PAIRS):
            pair_item(group).store().wait()
        for group in range(REST):
            rest_item(group).store().wait()


def front(owner, lengths, master, vectors, inputs, cotangent):
    rows, span = inputs.shape[0] // 2, inputs.shape[1]
    tokens = rows * LEN
    any_spec = pl.BlockSpec(memory_space=pl.ANY)
    smem = pl.BlockSpec(memory_space=pltpu.SMEM)
    whole = jax.ShapeDtypeStruct((rows, LEN, D), b16)
    dma = pltpu.SemaphoreType.DMA
    return pl.pallas_call(
        front_kernel,
        grid=(PAIRS, rows),
        in_specs=[
            smem,
            smem,
            pl.BlockSpec((CAP, HALF, D), lambda h, r: (0, 0, 0), pipeline_mode=pl.Buffered(1)),
            pl.BlockSpec((PIECES, D), lambda h, r: (0, 0)),
            any_spec,
            any_spec,
        ],
        out_specs=[any_spec] * 5
        + [
            pl.BlockSpec((PAIR, tokens), lambda h, r: (h, 0)),
            pl.BlockSpec((PAIR, tokens), lambda h, r: (h, 0)),
            pl.BlockSpec((tokens, PAIR), lambda h, r: (0, h)),
            pl.BlockSpec((2, LEN, LEN), lambda h, r: (h * 2 + r, 0, 0)),
            pl.BlockSpec((1, 2, LEN), lambda h, r: (h * 2 + r, 0, 0)),
            pl.BlockSpec((PAIR, LEN), lambda h, r: (h, r)),
            pl.BlockSpec((LEN, PAIR), lambda h, r: (r, h)),
        ],
        out_shape=[
            whole,
            whole,
            jax.ShapeDtypeStruct((tokens, D), b16),
            jax.ShapeDtypeStruct((PAIRS, D, WIDE), b16),
            jax.ShapeDtypeStruct((REST, D, D), b16),
            jax.ShapeDtypeStruct((D, tokens), b16),
            jax.ShapeDtypeStruct((D, tokens), b16),
            jax.ShapeDtypeStruct((tokens, D), b16),
            jax.ShapeDtypeStruct((rows * HEADS, LEN, LEN), b16),
            jax.ShapeDtypeStruct((rows * PAIRS, 2, LEN), f32),
            jax.ShapeDtypeStruct((D, tokens), b16),
            jax.ShapeDtypeStruct((tokens, D), b16),
        ],
        scratch_shapes=[
            pltpu.SMEM((PIECES,), jnp.int32),
            pltpu.VMEM((rows, LEN, D), b16),
            pltpu.VMEM((tokens, D), b16),
            pltpu.VMEM((tokens, PAIR), b16),
            pltpu.VMEM((PAIR, tokens), b16),
            pltpu.VMEM((2, LEN, LEN // 2), f32),
            pltpu.VMEM((CAP, HALF, D), b16),
        ]
        + [pltpu.VMEM((FLOWS, CAP, NEAR, wide * PAIR), b16) for unused, wide in GROUPS]
        + [pltpu.VMEM((FLOWS, 2 * CAP, KEEP, wide * PAIR), b16) for unused, wide in GROUPS]
        + [
            pltpu.VMEM((PAIRS, D, WIDE), b16),
            pltpu.VMEM((PAIRS, NEAR, WIDE), b16),
            pltpu.VMEM((2, PAIRS, NEAR, WIDE), b16),
            pltpu.VMEM((REST, D, D), b16),
            pltpu.VMEM((REST, NEAR, D), b16),
            pltpu.VMEM((2, REST, NEAR, D), b16),
            dma((CHUNKS, FLOWS, 3)),
            dma((CHUNKS, FLOWS, 3)),
            dma((PAIRS, 8)),
            dma((PAIRS, 8)),
            dma((REST, 8)),
            dma((REST, 8)),
            dma((2,)),
            dma((2,)),
            dma((2,)),
            dma((PAIRS + REST + 2,)),
        ],
        compiler_params=pltpu.CompilerParams(
            collective_id=0, has_side_effects=True, vmem_limit_bytes=60 * MIB
        ),
        name="front",
    )(owner, lengths, master, vectors, inputs, cotangent)


class Sum:
    steps = 7

    def __init__(self, place, work, kept, wide, narrow, land, sems, send_pair, add_own):
        self.place, self.work, self.kept, self.sems = place, work, kept, sems
        self.wide, self.narrow, self.land = wide, narrow, land
        self.send_pair, self.add_own = send_pair, add_own

    def copy(self, flow, index):
        first, second, near, far, keep, give = self.place.flow(flow)
        source, target, device = [
            (self.work.at[:, rows_at(far, NEAR)], self.wide.at[flow], first),
            (self.work.at[:, rows_at(give, KEEP)], self.narrow.at[flow], second),
        ][index]
        number = 3 + 2 * flow + index
        return remote(
            source,
            target,
            self.sems[0].at[number],
            self.sems[1].at[number],
            self.place.partners[device],
        )

    def step(self, index):
        if index == 0:
            self.send_pair().start()
        if index == 1:
            self.send_pair().wait()
            self.add_own()
        for flow in range(FLOWS):
            first, second, near, far, keep, give = self.place.flow(flow)
            if index == 1:
                self.copy(flow, 0).start()
            if index == 2:
                self.copy(flow, 0).wait()
                rows = rows_at(near, NEAR)
                total = self.work[:, rows].astype(f32) + self.wide[flow].astype(f32)
                self.work[:, rows] = total.astype(b16)
                self.copy(flow, 1).start()
            if index == 3:
                self.copy(flow, 1).wait()
                total = self.work[:, rows_at(keep, KEEP)].astype(f32) + self.narrow[flow].astype(f32)
                self.kept[:, both_flows(flow)] = total.astype(b16)
        if index >= 3:
            column_step(self.place, Column(self.place, self.kept, self.land, self.sems), index - 3)


class Gather:
    steps = 3

    def __init__(self, place, work, kept, narrow, wide, sems):
        self.place, self.work, self.kept = place, work, kept
        self.narrow, self.wide, self.sems = narrow, wide, sems

    def copy(self, flow, index):
        first, second, near, far, keep, give = self.place.flow(flow)
        source, target, device = [
            (self.kept.at[:, both_flows(flow)], self.narrow, second),
            (self.work.at[:, rows_at(near, NEAR)], self.wide, first),
        ][index]
        number = 7 + 2 * flow + index
        return remote(
            source,
            target.at[flow],
            self.sems[0].at[number],
            self.sems[1].at[number],
            self.place.partners[device],
        )

    def step(self, index):
        for flow in range(FLOWS):
            first, second, near, far, keep, give = self.place.flow(flow)
            if index == 0:
                self.work[:, rows_at(keep, KEEP)] = self.kept[:, both_flows(flow)]
            if index > 0:
                self.copy(flow, index - 1).wait()
            if index == 1:
                self.work[:, rows_at(give, KEEP)] = self.narrow[flow]
            if index == 2:
                self.work[:, rows_at(far, NEAR)] = self.wide[flow]
            if index < 2:
                self.copy(flow, index).start()


class Hand:
    steps = 3

    def __init__(self, place, table, kept, bag, gift, pack, last, own, out, sems, store_sems):
        self.place, self.table, self.kept = place, table, kept
        self.bag, self.gift, self.pack, self.last, self.own = bag, gift, pack, last, own
        self.out, self.sems, self.store_sems = out, sems, store_sems

    def tile(self, chip, rank, flow):
        return self.kept[self.table[chip * CAP + rank], both_flows(flow)]

    def copy(self, flow, index):
        first, second = self.place.flow(flow)[:2]
        source, target, device = [
            (self.bag.at[flow], self.gift.at[flow], second),
            (self.pack.at[flow], self.last.at[flow], first),
        ][index]
        return remote(
            source,
            target,
            self.sems[0].at[flow, index],
            self.sems[1].at[flow, index],
            self.place.partners[device],
        )

    def stores(self, flow):
        first, second, near, far, keep, give = self.place.flow(flow)
        parts = [
            (self.own.at[flow], rows_at(keep, KEEP)),
            (self.gift.at[flow, pl.ds(0, CAP)], rows_at(give, KEEP)),
            (self.last.at[flow], rows_at(far, NEAR)),
        ]
        return [
            pltpu.make_async_copy(source, self.out.at[:, rows], self.store_sems.at[flow, index])
            for index, (source, rows) in enumerate(parts)
        ]

    def step(self, index):
        for flow in range(FLOWS):
            first, second, near, far, keep, give = self.place.flow(flow)
            if index == 0:
                beside = self.place.chips[second]
                across = beside + self.place.chips[first] - self.place.me
                for rank in range(CAP):
                    self.bag[flow, rank] = self.tile(beside, rank, flow)
                    self.bag[flow, CAP + rank] = self.tile(across, rank, flow)
                    self.own[flow, rank] = self.tile(self.place.me, rank, flow)
                self.copy(flow, 0).start()
            if index == 1:
                self.copy(flow, 0).wait()
                for rank in range(CAP):
                    mine = self.tile(self.place.chips[first], rank, flow)
                    self.pack[flow, rank, rows_at(keep - near, KEEP)] = mine
                    self.pack[flow, rank, rows_at(give - near, KEEP)] = self.gift[flow, CAP + rank]
                self.copy(flow, 1).start()
            if index == 2:
                self.copy(flow, 1).wait()
                for copy in self.stores(flow):
                    copy.start()


BACK_STEPS = 2 * PAIRS
BACK_TAIL = 4
BACK_PAIRS = tuple((index, 1) for index in range(PAIRS))
BACK_REST = (0, 1, 2, 3, 4, 5, 6, 7, 8)
BACK_HAND = 15


def back_kernel(
    table, p_ref, r_ref, v_ref, q_ref, k_ref, o_ref, g_ref, w_ref, n_ref, x_ref, z_ref, vec_ref,
    tiles_in, sums_in, y_in,
    y_out, i_out, pairs_out, slots_out, sums_ref,
    grad_sum, wide_sum, turned, slopes, block_out,
    two, two_kept, two_wide, two_narrow, two_land, two_stage,
    one, one_kept, one_wide, one_narrow, one_land, one_send_stage, one_stage,
    gather_narrow, gather_wide,
    bag, gift, pack, last, own, vec_land,
    two_send, two_recv, one_send, one_recv, hand_send, hand_recv, hand_store,
    pair_two_send, pair_two_recv, pair_one_send, pair_one_recv, load_sem, store_sem,
    swap_send, swap_recv, swap_local, vec_send, vec_recv,
):
    step = pl.program_id(0)
    place = Place()
    rows, span = y_in.shape[0], y_in.shape[1] // 2
    near_half = rows_at(place.core * HALF, HALF)
    far_half = rows_at(place.other * HALF, HALF)

    def load_two(group):
        first, count = REST_GROUPS[group]
        return pltpu.make_async_copy(
            tiles_in.at[pl.ds(first, count), near_half],
            two_stage.at[pl.ds(group % 2, 1)],
            load_sem.at[group % 2],
        )

    def rest_sum(group):
        first, count = REST_GROUPS[group]
        span_of = pl.ds(first, count)
        work = two.at[span_of]

        def send_pair():
            return remote(
                tiles_in.at[span_of, far_half],
                work,
                pair_two_send.at[group],
                pair_two_recv.at[group],
                place.twin,
            )

        def add_own():
            load_two(group).wait()
            work[...] = (work[...].astype(f32) + two_stage[group % 2].astype(f32)).astype(b16)

        sems = (two_send.at[group], two_recv.at[group])
        parts = (two_kept.at[span_of], two_wide.at[:, span_of], two_narrow.at[:, span_of])
        return Sum(place, work, *parts, two_land.at[:, span_of], sems, send_pair, add_own)

    def pair_sum(group):
        first, count = BACK_PAIRS[group]
        span_of = pl.ds(first, count)
        work = one.at[span_of]

        def send_pair():
            return remote(
                one_send_stage.at[pl.ds(group % 2, 1)],
                work,
                pair_one_send.at[group],
                pair_one_recv.at[group],
                place.twin,
            )

        def add_own():
            own = one_stage[group % 2].astype(f32)
            work[...] = (work[...].astype(f32) + own).astype(b16)

        sems = (one_send.at[group], one_recv.at[group])
        parts = (one_kept.at[span_of], one_wide.at[:, span_of], one_narrow.at[:, span_of])
        return Sum(place, work, *parts, one_land.at[:, span_of], sems, send_pair, add_own)

    def pair_gather(group):
        first, count = BACK_PAIRS[group]
        span_of = pl.ds(first, count)
        sems = (one_send.at[group], one_recv.at[group])
        narrow, wide = gather_narrow.at[:, span_of], gather_wide.at[:, span_of]
        return Gather(place, one.at[span_of], one_kept.at[span_of], narrow, wide, sems)

    hand = Hand(
        place, table, two_kept, bag, gift, pack, last, own, slots_out, (hand_send, hand_recv), hand_store
    )

    def pair_store(index, tile):
        return pltpu.make_async_copy(
            one.at[index, :, pl.ds(tile * PAIR, PAIR)],
            pairs_out.at[tile, :, pl.ds(index * PAIR, PAIR)],
            store_sem.at[index, tile],
        )

    def tick(number, odd):
        for group, start in enumerate(BACK_REST):
            if group % 2 == odd and 0 <= number - start < Sum.steps:
                rest_sum(group).step(number - start)
        for group, (first, count) in enumerate(BACK_PAIRS):
            if group % 2 != odd:
                continue
            start = 2 * (first + count)
            if 0 <= number - start < Sum.steps:
                pair_sum(group).step(number - start)
            if 0 <= number - start - Sum.steps + 1 < Gather.steps:
                pair_gather(group).step(number - start - Sum.steps + 1)
            if number == start + Sum.steps + 1:
                for index in range(first, first + count):
                    for tile in range(3):
                        pair_store(index, tile).start()
        if odd == 0 and 0 <= number - BACK_HAND < Hand.steps:
            hand.step(number - BACK_HAND)
        for group, start in enumerate(BACK_REST):
            if odd == 1 and number == max(start - 1, 0):
                load_two(group).start()

    def both(number):
        tick(number, 0)
        tick(number, 1)

    def swap_y(index):
        there = pl.ds(place.core * rows, rows)
        if index == 0:
            return pltpu.make_async_copy(
                y_in.at[:, pl.ds(place.core * span, span)], y_out.at[there], swap_local.at[0]
            )
        return remote(
            y_in.at[:, pl.ds(place.other * span, span)],
            y_out.at[there],
            swap_send.at[0],
            swap_recv.at[0],
            place.twin,
        )

    @pl.when(step == 0)
    def lead():
        place.greet()
        for index in range(2):
            swap_y(index).start()
        sums_ref[...] = sums_in[...]

    for number in range(BACK_STEPS + BACK_TAIL):
        early = partial(tick, number, 0) if number < BACK_STEPS else partial(both, number)
        pl.when(step == number)(early)

    half = LEN // 2
    pair, row = step // 2, lax.rem(step, 2)

    quarter = LEN // 4

    def attention_inputs(head):
        part = slice(head * HEAD_DIM, (head + 1) * HEAD_DIM)
        values = head_only(v_ref[...], head)
        recip = r_ref[0, head : head + 1, :]
        grad = g_ref[part, :].astype(f32) * recip
        delta = jnp.sum(grad * o_ref[part, :].astype(f32), 0, keepdims=True)
        grad = grad.astype(b16)
        return values, grad, delta, jnp.concatenate([grad, grad], axis=0)

    def attention(head):
        part = slice(head * HEAD_DIM, (head + 1) * HEAD_DIM)
        values, grad, delta, doubled = attention_inputs(head)
        units = [(which, block) for which in range(2) for block in range(4)]
        value_grad, key_grad, query_grad = {}, {}, {}

        def raw_block(unit):
            which, block = units[unit]
            cols = slice(which * half, (which + 1) * half)
            return dot_nn(values[block * quarter : (block + 1) * quarter], doubled[:, cols])

        def slope_block(unit, raw):
            which, block = units[unit]
            cols = slice(which * half, (which + 1) * half)
            for small in range(4):
                rows_here = slice(small * 64, (small + 1) * 64)
                rows_all = slice(block * quarter + small * 64, block * quarter + (small + 1) * 64)
                slope = p_ref[head, rows_all, cols].astype(f32) * (raw[rows_here] - delta[:, cols])
                slopes[unit % 2, rows_here] = slope.astype(b16)

        def add(totals, key, term):
            totals[key] = totals[key] + term if key in totals else term

        def grad_block(unit):
            which, block = units[unit]
            cols = slice(which * half, (which + 1) * half)
            rows_all = slice(block * quarter, (block + 1) * quarter)
            slope = slopes[unit % 2]
            add(value_grad, block, dot_nt(grad[:, cols], p_ref[head, rows_all, cols]))
            add(key_grad, block, dot_nt(q_ref[part, cols], slope))
            add(query_grad, which, dot_nn(k_ref[part, rows_all], slope))

        raw = raw_block(0)
        for unit in range(len(units)):
            after = raw_block(unit + 1) if unit + 1 < len(units) else None
            slope_block(unit, raw)
            if unit > 0:
                grad_block(unit - 1)
            raw = after
        grad_block(len(units) - 1)
        for which in range(2):
            total = query_grad[which] * (HEAD_DIM**-0.5)
            turned[part, which * half : (which + 1) * half] = total.astype(b16)
        for block in range(4):
            rows_all = slice(block * quarter, (block + 1) * quarter)
            lower = slice(PAIR + head * HEAD_DIM, PAIR + (head + 1) * HEAD_DIM)
            turned[lower, rows_all] = (key_grad[block] * (1.0 / LOG2E)).astype(b16)
            lower = slice(2 * PAIR + head * HEAD_DIM, 2 * PAIR + (head + 1) * HEAD_DIM)
            turned[lower, rows_all] = value_grad[block].astype(b16)

    @pl.when(step < BACK_STEPS)
    def first_head():
        attention(0)

    for number in range(BACK_STEPS):
        pl.when(step == number)(partial(tick, number, 1))

    @pl.when(step < BACK_STEPS)
    def second_head():
        attention(1)
        where = pl.ds(pl.multiple_of(row * LEN, LEN), LEN)
        block = dot_nn(turned[...], n_ref[where])
        back = turned[...].T
        lanes = pl.ds(pl.multiple_of(pair * PAIR, PAIR), PAIR)
        ones = jnp.sum(back.astype(f32), 0, keepdims=True)
        sums_ref[4:5, lanes] += ones[:, :PAIR]
        sums_ref[5:6, lanes] += ones[:, 2 * PAIR :]
        term = dot_nt(back, w_ref[0])

        @pl.when(pair == 0)
        def begin():
            grad_sum[where] = term

        @pl.when(pair > 0)
        def add():
            grad_sum[where] += term

        @pl.when(row == 0)
        def keep():
            wide_sum[...] = block

        @pl.when(row == 1)
        def hand_on():
            whole = (wide_sum[...] + block).T
            low = whole.astype(b16)
            for core in range(2):

                @pl.when(place.core == core)
                def split():
                    slot = lax.rem(pair, 2)
                    one_stage[slot] = low[core * HALF : (core + 1) * HALF]
                    one_send_stage[slot] = low[(1 - core) * HALF : (2 - core) * HALF]

    def store_block(index):
        row, half = index // 2, index % 2
        target = i_out.at[place.core * rows + row]
        local = pltpu.make_async_copy(block_out.at[half], target, swap_local.at[1 + row])
        far = remote(
            block_out.at[half], target, swap_send.at[1 + row], swap_recv.at[1 + row], place.twin
        )
        return local, far, half

    def wait_block(index):
        local, far, half = store_block(index)

        @pl.when(place.core == half)
        def keep():
            local.wait()

        @pl.when(place.core != half)
        def give():
            far.wait()

    for index in range(BACK_TAIL):

        @pl.when(step == BACK_STEPS + index)
        def close():
            size = LEN // 2
            if index >= 2:
                wait_block(index - 2)
            gain_sum = jnp.zeros((8, D), f32)
            shift_sum = jnp.zeros((8, D), f32)
            for block in range(size // 16):
                rows_here = slice(block * 16, (block + 1) * 16)
                grad = grad_sum[index * size + block * 16 : index * size + (block + 1) * 16]
                unit, rstd = norm_parts(x_ref[rows_here].astype(f32))
                gain_sum = gain_sum + jnp.sum((grad * unit).reshape(-1, 8, D), axis=0)
                shift_sum = shift_sum + jnp.sum(grad.reshape(-1, 8, D), axis=0)
                total = norm_back(grad, unit, rstd, vec_ref[0:1, :])
                block_out[index % 2, rows_here] = (z_ref[rows_here].astype(f32) + total).astype(b16)
            sums_ref[0:1, :] += jnp.sum(gain_sum, 0, keepdims=True)
            sums_ref[1:2, :] += jnp.sum(shift_sum, 0, keepdims=True)
            local, far, half = store_block(index)

            @pl.when(place.core == half)
            def keep():
                local.start()

            @pl.when(place.core != half)
            def give():
                far.start()

    @pl.when(step == BACK_STEPS + BACK_TAIL - 1)
    def drain():
        devices = [place.twin] + place.partners

        def vector(index):
            return remote(
                sums_ref, vec_land.at[index], vec_send.at[index], vec_recv.at[index], devices[index]
            )

        vector(0).start()
        for number in range(BACK_STEPS + BACK_TAIL, BACK_STEPS + Sum.steps + Gather.steps):
            both(number)
            index = number - BACK_STEPS - BACK_TAIL
            if index < 5:
                vector(index).wait()
                sums_ref[...] += vec_land[index]
                if index < 4:
                    vector(index + 1).start()
        for index in range(2):
            swap_y(index).wait()
        for index in range(2, BACK_TAIL):
            wait_block(index)
        for index in range(PAIRS):
            for tile in range(3):
                pair_store(index, tile).wait()
        for flow in range(FLOWS):
            for copy in hand.stores(flow):
                copy.wait()


def back(table, attention, weights, normed, x, residual, vectors, tiles, sums, y):
    rows, length = y.shape[:2]
    tokens = rows * length
    any_spec = pl.BlockSpec(memory_space=pl.ANY)
    smem = pl.BlockSpec(memory_space=pltpu.SMEM)
    dma = pltpu.SemaphoreType.DMA

    def now(step):
        return jnp.minimum(step, BACK_STEPS - 1)

    def tail(step):
        return jnp.maximum(step - BACK_STEPS, 0)

    head_block = pl.BlockSpec((PAIR, LEN), lambda s: (now(s) // 2, lax.rem(now(s), 2)))
    tail_block = pl.BlockSpec((LEN // 2, D), lambda s: (tail(s), 0))
    whole = pl.BlockSpec((PIECES, D), lambda s: (0, 0))
    sums_block = pl.BlockSpec((16, D), lambda s: (0, 0))
    return pl.pallas_call(
        back_kernel,
        grid=(BACK_STEPS + BACK_TAIL,),
        in_specs=[
            smem,
            pl.BlockSpec((2, LEN, LEN), lambda s: (now(s), 0, 0)),
            pl.BlockSpec((1, 2, LEN), lambda s: (now(s), 0, 0)),
            pl.BlockSpec((LEN, PAIR), lambda s: (lax.rem(now(s), 2), now(s) // 2)),
            head_block,
            head_block,
            head_block,
            head_block,
            pl.BlockSpec((1, D, WIDE), lambda s: (now(s) // 2, 0, 0)),
            pl.BlockSpec((tokens, D), lambda s: (0, 0), pipeline_mode=pl.Buffered(1)),
            tail_block,
            tail_block,
            whole,
            any_spec,
            sums_block,
            any_spec,
        ],
        out_specs=[any_spec] * 4 + [sums_block],
        out_shape=[
            jax.ShapeDtypeStruct((2 * rows, length // 2, D), b16),
            jax.ShapeDtypeStruct((2 * rows, length // 2, D), b16),
            jax.ShapeDtypeStruct((3, HALF, D), b16),
            jax.ShapeDtypeStruct((CAP, HALF, D), b16),
            jax.ShapeDtypeStruct((16, D), f32),
        ],
        scratch_shapes=[
            pltpu.VMEM((tokens, D), f32),
            pltpu.VMEM((WIDE, D), f32),
            pltpu.VMEM((WIDE, LEN), b16),
            pltpu.VMEM((2, LEN // 4, LEN // 2), b16),
            pltpu.VMEM((2, LEN // 2, D), b16),
            pltpu.VMEM((REST, HALF, D), b16),
            pltpu.VMEM((REST, NEAR, D), b16),
            pltpu.VMEM((FLOWS, REST, NEAR, D), b16),
            pltpu.VMEM((FLOWS, REST, KEEP, D), b16),
            pltpu.VMEM((2, REST, NEAR, D), b16),
            pltpu.VMEM((2, HALF, D), b16),
            pltpu.VMEM((PAIRS, HALF, WIDE), b16),
            pltpu.VMEM((PAIRS, NEAR, WIDE), b16),
            pltpu.VMEM((FLOWS, PAIRS, NEAR, WIDE), b16),
            pltpu.VMEM((FLOWS, PAIRS, KEEP, WIDE), b16),
            pltpu.VMEM((2, PAIRS, NEAR, WIDE), b16),
            pltpu.VMEM((2, HALF, WIDE), b16),
            pltpu.VMEM((2, HALF, WIDE), b16),
            pltpu.VMEM((FLOWS, PAIRS, KEEP, WIDE), b16),
            pltpu.VMEM((FLOWS, PAIRS, NEAR, WIDE), b16),
            pltpu.VMEM((FLOWS, 2 * CAP, KEEP, D), b16),
            pltpu.VMEM((FLOWS, 2 * CAP, KEEP, D), b16),
            pltpu.VMEM((FLOWS, CAP, NEAR, D), b16),
            pltpu.VMEM((FLOWS, CAP, NEAR, D), b16),
            pltpu.VMEM((FLOWS, CAP, KEEP, D), b16),
            pltpu.VMEM((5, 16, D), f32),
            dma((REST, 7)),
            dma((REST, 7)),
            dma((PAIRS, 11)),
            dma((PAIRS, 11)),
            dma((FLOWS, 2)),
            dma((FLOWS, 2)),
            dma((FLOWS, 3)),
            dma((REST,)),
            dma((REST,)),
            dma((PAIRS,)),
            dma((PAIRS,)),
            dma((3,)),
            dma((PAIRS, 3)),
            dma((3,)),
            dma((3,)),
            dma((3,)),
            dma((5,)),
            dma((5,)),
        ],
        compiler_params=pltpu.CompilerParams(
            collective_id=1, has_side_effects=True, vmem_limit_bytes=62 * MIB
        ),
        name="back",
    )(table, *attention, weights, normed, x, residual, vectors, tiles, sums, y)


def update_kernel(tile_at, one, two, w_ref, m_ref, s_ref, y_in, i_in, w_out, m_out, s_out, y_out, i_out):
    step = pl.program_id(0)
    tile = tile_at[step // 2]
    grad = jnp.where(tile < 3, one[0], two[0]).astype(f32)
    parts = adam_step(w_ref[0], grad, m_ref[0], s_ref[0], RATE)
    for target, part in zip((w_out, m_out, s_out), parts):
        target[0] = jnp.where(tile >= 0, part, jnp.zeros_like(part))

    @pl.when(step < 4)
    def widen():
        y_out[...] = y_in[...].astype(f32)
        i_out[...] = i_in[...].astype(f32)


def update(tile_at, one, two, master, first, second, y, grad):
    tokens = y.shape[0]
    size = HALF // 2
    state = pl.BlockSpec((1, size, D), lambda s, tile_at: (s // 2, lax.rem(s, 2), 0))
    wide = pl.BlockSpec((tokens // 4, D), lambda s, tile_at: (jnp.minimum(s, 3), 0))
    return pl.pallas_call(
        update_kernel,
        grid_spec=pltpu.PrefetchScalarGridSpec(
            num_scalar_prefetch=1,
            grid=(CAP * 2,),
            in_specs=[
                pl.BlockSpec(
                    (1, size, D),
                    lambda s, tile_at: (jnp.clip(tile_at[s // 2], 0, 2), lax.rem(s, 2), 0),
                ),
                state,
                state,
                state,
                state,
                wide,
                wide,
            ],
            out_specs=[state] * 3 + [wide] * 2,
        ),
        out_shape=[jax.ShapeDtypeStruct(master.shape, f32)] * 3
        + [jax.ShapeDtypeStruct((tokens, D), f32)] * 2,
        compiler_params=pltpu.CompilerParams(vmem_limit_bytes=60 * MIB),
        name="update",
    )(tile_at, one, two, master, first, second, y, grad)


def shards_paired(
    inputs,
    cotangent,
    doc_lengths,
    owner_list,
    master,
    first_moment,
    second_moment,
    vectors,
    vector_first,
    vector_second,
):
    rows_here, span, width = inputs.shape
    place = lax.axis_index("blk")
    member = lax.axis_index("dp")
    rows_mine = rows_here // 2
    order = jnp.arange(PIECES)
    same_owner = owner_list[:, None] == owner_list[None, :]
    ranks = jnp.sum(same_owner & (order[None, :] < order[:, None]), axis=1).astype(jnp.int32)
    slot_of = owner_list * CAP + ranks
    front_outs = front(owner_list, doc_lengths, master, vectors, inputs, cotangent)
    x, cot, normed, weights_one, weights_two, queries, keys, values = front_outs[:8]
    weights, recips, context_turned, context = front_outs[8:]
    x = x.reshape(-1, width)
    cot = cot.reshape(-1, width)
    block_out, residual, grad_context, sums, tiles_two = feed(
        context, context_turned, x, cot, weights_two, vectors
    )
    hits = jnp.arange(16 * CAP)[:, None] == slot_of[None, :]
    tile_at = jnp.sum(jnp.where(hits, order[None, :] + 1, 0), axis=1).astype(jnp.int32) - 1
    table = jnp.maximum(tile_at - 3, 0)
    block_out, input_grad, total_one, total_two, vector_total = back(
        table,
        (weights, recips, values, queries, keys, context_turned, grad_context),
        weights_one,
        normed,
        x,
        residual,
        vectors,
        tiles_two,
        sums,
        block_out.reshape(rows_mine, LEN, width),
    )
    mine = lax.dynamic_slice_in_dim(tile_at, member * CAP, CAP, 0)
    *updated, block_out, input_grad = update(
        mine,
        total_one,
        total_two,
        master,
        first_moment,
        second_moment,
        block_out.reshape(-1, width),
        input_grad.reshape(-1, width),
    )
    columns = vector_first.shape[1]
    vector_cols = lax.dynamic_slice_in_dim(vectors, place * columns, columns, 1)
    vector_total = lax.dynamic_slice(vector_total, (0, place * columns), (PIECES, columns))
    updated_vectors = adam_step(vector_cols, vector_total, vector_first, vector_second, VEC_RATE)
    return (
        block_out.reshape(inputs.shape),
        input_grad.reshape(inputs.shape),
        *updated,
        *updated_vectors,
    )


def solution(mesh):
    in_specs = (
        P("dp", "blk", None),
        P("dp", "blk", None),
        P("dp", None),
        P(),
        P("dp", "blk", None),
        P("dp", "blk", None),
        P("dp", "blk", None),
        P(),
        P(None, "blk"),
        P(None, "blk"),
    )
    out_specs = (
        P("dp", "blk", None),
        P("dp", "blk", None),
        P("dp", "blk", None),
        P("dp", "blk", None),
        P("dp", "blk", None),
        P(None, "blk"),
        P(None, "blk"),
        P(None, "blk"),
    )
    paired = mesh.shape["blk"] == 2 and mesh.shape["dp"] == 16
    shards = shards_paired if paired else shards_any
    return jax.shard_map(shards, mesh=mesh, in_specs=in_specs, out_specs=out_specs, check_vma=False)
```

profile of v0, /device:TPU:0, one launch (start us, length us, event | category | flops | bytes accessed | tf_op | source)
XLA Modules:
  0.0 400.4 jit_solution(2506272672456931439)
XLA Ops:
  0.6 1.3 copy.19.lengths
  2.0 129.5 %front.1 = (bf16[2,1024,768]{2,1,0:T(8,128)(2,1)}, bf16[2,1024,768]{2,1,0:T(8,128)(2,1)}, bf16[2048,768]{1,0:T(8,128)(2,1)}, bf16[6,768,384]{2,1,0:T(8,128)(2,1)...) custom-call(s32[12]{0:T(128)} %owner.1, ...), custom_call_target="tpu_custom_call" | custom-call | tf_op jit(solution)/shard_map/front/pallas_call | solution.py:882
  131.4 0.0 copy-start.4
  131.5 96.0 %feed.1 = (bf16[2048,768]{1,0:T(8,128)(2,1)}, bf16[2048,768]{1,0:T(8,128)(2,1)}, bf16[768,2048]{1,0:T(8,128)(2,1)}, f32[16,768]{1,0:T(8,128)}, bf16[9,768,768]{2,1,0:T(8,128)(2,1)}) custom-call(bf16[2048,768]{1,0:T(8,128)(2,1)} %get-tuple-element.41.c_ref, bf16[768,2048]{1,0:T(8,128)(2,1)} %get-tuple-element.40.o_ref, bf16[2048,768]{1,0:T(8,128)(2,1)} %bitcast.7, ...), custom_call_target="tpu_custom_call" | custom-call | flops 65229815808 | bytes 49545216 | tf_op jit(solution)/shard_map/feed/pallas_call | solution.py:402
  227.5 0.0 copy-done.4
  227.5 0.2 convert_reduce_fusion
  227.7 0.1 select_reduce_fusion
  227.8 0.5 add_maximum_fusion
  228.3 153.3 %back.1 = (bf16[4,512,768]{2,1,0:T(8,128)(2,1)}, bf16[4,512,768]{2,1,0:T(8,128)(2,1)}, bf16[3,384,768]{2,1,0:T(8,128)(2,1)}, bf16[3,384,768]{2,1,0:T(8,128)(2,1)}, f32[16,768]{1,0:T(8,128)}) custom-call(s32[48]{0:T(128)} %get-tuple-element.65.table, bf16[24,1024,1024]{2,1,0:T(8,128)(2,1)} %get-tuple-element.35.p_ref, ...), custom_call_target="tpu_custom_call" | custom-call | tf_op jit(solution)/shard_map/back/pallas_call | solution.py:1448
  381.6 0.6 dynamic_slice.9.tile_at
  382.2 0.0 copy-start
  382.2 0.0 copy-start.1
  382.2 0.0 copy-start.2
  382.2 0.0 copy-start.3
  382.2 17.3 %update.1 = (f32[3,384,768]{2,1,0:T(8,128)}, f32[3,384,768]{2,1,0:T(8,128)}, f32[3,384,768]{2,1,0:T(8,128)}, f32[2048,768]{1,0:T(8,128)}, f32[2048,768]{1,0:T(8,128)}) custom-call(s32[3]{0:T(128)} %dynamic_slice.9.tile_at, bf16[3,384,768]{2,1,0:T(8,128)(2,1)} %get-tuple-element.52.one, bf16[3,384,768]{2,1,0:T(8,128)(2,1)} %get-tuple-element.53.two, ...), custom_call_target="tpu_custom_call" | custom-call | tf_op jit(solution)/shard_map/update/pallas_call | solution.py:1549
  399.5 0.0 copy-done
  399.5 0.0 copy-done.1
  399.5 0.0 copy-done.2
  399.5 0.0 copy-done.3
  399.5 0.6 multiply_subtract_fusion
  (1 shorter events, 0.0 us)
Async XLA Ops:
  131.4 96.1 %copy-start.4 = (s32[12]{0:T(128)S(1)}, s32[12]{0:T(128)}, u32[]{:S(2)}) copy-start(s32[12]{0:T(128)} %owner.1) | copy-start | bytes 148
  382.2 17.3 %copy-start = (f32[12,768]{1,0:T(8,128)S(1)}, f32[12,768]{1,0:T(8,128)}, u32[]{:S(2)}) copy-start(f32[12,768]{1,0:T(8,128)} %vec_ref.5) | copy-start | bytes 110596
  382.2 17.3 %copy-start.1 = (f32[12,384]{1,0:T(8,128)S(1)}, f32[12,384]{1,0:T(8,128)}, u32[]{:S(2)}) copy-start(f32[12,384]{1,0:T(8,128)} %param.18) | copy-start | bytes 55300
  382.2 17.3 %copy-start.2 = (f32[12,384]{1,0:T(8,128)S(1)}, f32[12,384]{1,0:T(8,128)}, u32[]{:S(2)}) copy-start(f32[12,384]{1,0:T(8,128)} %param.19) | copy-start | bytes 55300
  382.2 17.3 %copy-start.3 = (f32[16,768]{1,0:T(8,128)S(1)}, f32[16,768]{1,0:T(8,128)}, u32[]{:S(2)}) copy-start(f32[16,768]{1,0:T(8,128)} %get-tuple-element.61) | copy-start | bytes 147460
where the time goes:
time: 401 us; the launch traced here: 400 us
  Pallas kernels  396 us (99%)
    pallas_call x1, Pallas kernels, back(): pl.pallas_call(back_kernel, grid=(BACK_STEPS + BACK_TAIL,), in_specs=[sme...  153 us
    pallas_call x1, Pallas kernels, front(): pl.pallas_call(front_kernel, grid=(PAIRS, rows), in_specs=[smem, smem, pl...  129 us
    pallas_call x1, Pallas kernels, feed(): pl.pallas_call(feed_kernel, grid=(tokens // size,), in_specs=[token_block...  96 us
    pallas_call x1, Pallas kernels, update(): pl.pallas_call(update_kernel, grid_spec=pltpu.PrefetchScalarGridSpec(num_...  17.3 us

commit v1 on v0

--- a/solution.py
+++ b/solution.py
@@ -649,6 +649,7 @@
 FRONT_PAIRS = (2, 4, 5, 6, 7, 8)
 FRONT_REST = (6, 7, 8, 9, 10, 11, 12, 13, 14)
 FRONT_LEAD = 9
+FRONT_PHASES = 4
 
 
 def front_kernel(
@@ -723,19 +724,20 @@
         sems = (two_send.at[group], two_recv.at[group])
         return Item(place, two.at[span_of], two_kept.at[span_of], two_land.at[:, span_of], sems, load, store)
 
-    def tick(number, odd):
+    def tick(number, phase):
         for chunk in range(CHUNKS):
-            if odd == 0 and 0 <= number - 2 * chunk <= 2:
+            if phase == 0 and 0 <= number - 2 * chunk <= 2:
                 spread.step(chunk, number - 2 * chunk)
-        starts = [(pair_item, group, start) for group, start in enumerate(FRONT_PAIRS)]
-        starts += [(rest_item, group, start) for group, start in enumerate(FRONT_REST)]
-        for make, group, start in starts:
-            if group % 2 == odd and 0 <= number - start < Item.steps:
-                make(group).step(number - start)
+        for index, start in enumerate(FRONT_PAIRS):
+            if index % 2 * 2 == phase and 0 <= number - start < Item.steps:
+                pair_item(index).step(number - start)
+        for index, start in enumerate(FRONT_REST):
+            if (index + 1) % FRONT_PHASES == phase and 0 <= number - start < Item.steps:
+                rest_item(index).step(number - start)
 
     def both(number):
-        tick(number, 0)
-        tick(number, 1)
+        for phase in range(FRONT_PHASES):
+            tick(number, phase)
 
     @pl.when(grid_step == 0)
     def lead():
@@ -833,9 +835,9 @@
         peak = score_block(0, block, peak)
     before = None
     for unit, (head, step) in enumerate(units):
-        if unit == 2:
+        if unit > 0:
             for number in range(2 * PAIRS):
-                pl.when(grid_step == number)(partial(tick, FRONT_LEAD + number, 1))
+                pl.when(grid_step == number)(partial(tick, FRONT_LEAD + number, unit))
         here = slice(step * half, (step + 1) * half)
         top = jnp.max(peak, 0, keepdims=True)
         total = jnp.zeros((8, half), f32)
@@ -1100,6 +1102,7 @@
 BACK_PAIRS = tuple((index, 1) for index in range(PAIRS))
 BACK_REST = (0, 1, 2, 3, 4, 5, 6, 7, 8)
 BACK_HAND = 15
+BACK_PHASES = 3
 
 
 def back_kernel(
@@ -1191,31 +1194,30 @@
             store_sem.at[index, tile],
         )
 
-    def tick(number, odd):
-        for group, start in enumerate(BACK_REST):
-            if group % 2 == odd and 0 <= number - start < Sum.steps:
-                rest_sum(group).step(number - start)
-        for group, (first, count) in enumerate(BACK_PAIRS):
-            if group % 2 != odd:
+    def tick(number, phase):
+        for index, start in enumerate(BACK_REST):
+            if (index + 1) % BACK_PHASES == phase and 0 <= number - start < Sum.steps:
+                rest_sum(index).step(number - start)
+        for index in range(PAIRS):
+            start = 2 * index + 2
+            if index % 2 != phase:
                 continue
-            start = 2 * (first + count)
             if 0 <= number - start < Sum.steps:
-                pair_sum(group).step(number - start)
+                pair_sum(index).step(number - start)
             if 0 <= number - start - Sum.steps + 1 < Gather.steps:
-                pair_gather(group).step(number - start - Sum.steps + 1)
+                pair_gather(index).step(number - start - Sum.steps + 1)
             if number == start + Sum.steps + 1:
-                for index in range(first, first + count):
-                    for tile in range(3):
-                        pair_store(index, tile).start()
-        if odd == 0 and 0 <= number - BACK_HAND < Hand.steps:
+                for tile in range(3):
+                    pair_store(index, tile).start()
+        if phase == 0 and 0 <= number - BACK_HAND < Hand.steps:
             hand.step(number - BACK_HAND)
-        for group, start in enumerate(BACK_REST):
-            if odd == 1 and number == max(start - 1, 0):
-                load_two(group).start()
+        for index, start in enumerate(BACK_REST):
+            if phase == BACK_PHASES - 1 and number == max(start - 1, 0):
+                load_two(index).start()
 
     def both(number):
-        tick(number, 0)
-        tick(number, 1)
+        for phase in range(BACK_PHASES):
+            tick(number, phase)
 
     def swap_y(index):
         there = pl.ds(place.core * rows, rows)
@@ -1316,6 +1318,12 @@
     @pl.when(step < BACK_STEPS)
     def second_head():
         attention(1)
+
+    for number in range(BACK_STEPS):
+        pl.when(step == number)(partial(tick, number, 2))
+
+    @pl.when(step < BACK_STEPS)
+    def weight_grads():
         where = pl.ds(pl.multiple_of(row * LEN, LEN), LEN)
         block = dot_nn(turned[...], n_ref[where])
         back = turned[...].T

time: 401 us -> 402 us (level)
    pallas_call x1, Pallas kernels: 153 us -> 158 us  [back(): pl.pallas_call(back_kernel, grid=(BACK_STEPS + BACK_TAIL,), in_specs=[sme...]
where the time goes in v1:
time: 402 us
  Pallas kernels  397 us (99%)
    pallas_call x1, Pallas kernels, back(): pl.pallas_call(back_kernel, grid=(BACK_STEPS + BACK_TAIL,), in_specs=[sme...  158 us
    pallas_call x1, Pallas kernels, front(): pl.pallas_call(front_kernel, grid=(PAIRS, rows), in_specs=[smem, smem, pl...  126 us
    pallas_call x1, Pallas kernels, feed(): pl.pallas_call(feed_kernel, grid=(tokens // size,), in_specs=[token_block...  96 us
    pallas_call x1, Pallas kernels, update(): pl.pallas_call(update_kernel, grid_spec=pltpu.PrefetchScalarGridSpec(num_...  17.3 us

profile of v1, /device:TPU:0, one launch (start us, length us, event | category | flops | bytes accessed | tf_op | source)
XLA Modules:
  0.0 401.6 jit_solution(18250271757891222869)
XLA Ops:
  0.6 1.3 copy.19.lengths
  2.0 126.2 %front.1 = (bf16[2,1024,768]{2,1,0:T(8,128)(2,1)}, bf16[2,1024,768]{2,1,0:T(8,128)(2,1)}, bf16[2048,768]{1,0:T(8,128)(2,1)}, bf16[6,768,384]{2,1,0:T(8,128)(2,1)...) custom-call(s32[12]{0:T(128)} %owner.1, ...), custom_call_target="tpu_custom_call" | custom-call | tf_op jit(solution)/shard_map/front/pallas_call | solution.py:884
  128.2 0.0 copy-start.4
  128.2 96.0 %feed.1 = (bf16[2048,768]{1,0:T(8,128)(2,1)}, bf16[2048,768]{1,0:T(8,128)(2,1)}, bf16[768,2048]{1,0:T(8,128)(2,1)}, f32[16,768]{1,0:T(8,128)}, bf16[9,768,768]{2,1,0:T(8,128)(2,1)}) custom-call(bf16[2048,768]{1,0:T(8,128)(2,1)} %get-tuple-element.41.c_ref, bf16[768,2048]{1,0:T(8,128)(2,1)} %get-tuple-element.40.o_ref, bf16[2048,768]{1,0:T(8,128)(2,1)} %bitcast.7, ...), custom_call_target="tpu_custom_call" | custom-call | flops 65229815808 | bytes 49545216 | tf_op jit(solution)/shard_map/feed/pallas_call | solution.py:402
  224.2 0.0 copy-done.4
  224.2 0.2 convert_reduce_fusion
  224.4 0.1 select_reduce_fusion
  224.5 0.5 add_maximum_fusion
  225.0 157.8 %back.1 = (bf16[4,512,768]{2,1,0:T(8,128)(2,1)}, bf16[4,512,768]{2,1,0:T(8,128)(2,1)}, bf16[3,384,768]{2,1,0:T(8,128)(2,1)}, bf16[3,384,768]{2,1,0:T(8,128)(2,1)}, f32[16,768]{1,0:T(8,128)}) custom-call(s32[48]{0:T(128)} %get-tuple-element.65.table, bf16[24,1024,1024]{2,1,0:T(8,128)(2,1)} %get-tuple-element.35.p_ref, ...), custom_call_target="tpu_custom_call" | custom-call | tf_op jit(solution)/shard_map/back/pallas_call | solution.py:1456
  382.9 0.6 dynamic_slice.9.tile_at
  383.4 0.0 copy-start
  383.4 0.0 copy-start.1
  383.4 0.0 copy-start.2
  383.5 0.0 copy-start.3
  383.5 17.3 %update.1 = (f32[3,384,768]{2,1,0:T(8,128)}, f32[3,384,768]{2,1,0:T(8,128)}, f32[3,384,768]{2,1,0:T(8,128)}, f32[2048,768]{1,0:T(8,128)}, f32[2048,768]{1,0:T(8,128)}) custom-call(s32[3]{0:T(128)} %dynamic_slice.9.tile_at, bf16[3,384,768]{2,1,0:T(8,128)(2,1)} %get-tuple-element.52.one, bf16[3,384,768]{2,1,0:T(8,128)(2,1)} %get-tuple-element.53.two, ...), custom_call_target="tpu_custom_call" | custom-call | tf_op jit(solution)/shard_map/update/pallas_call | solution.py:1557
  400.7 0.0 copy-done
  400.7 0.0 copy-done.1
  400.7 0.0 copy-done.2
  400.8 0.0 copy-done.3
  400.8 0.6 multiply_subtract_fusion
  (1 shorter events, 0.0 us)
Async XLA Ops:
  128.2 96.1 %copy-start.4 = (s32[12]{0:T(128)S(1)}, s32[12]{0:T(128)}, u32[]{:S(2)}) copy-start(s32[12]{0:T(128)} %owner.1) | copy-start | bytes 148
  383.4 17.3 %copy-start = (f32[12,768]{1,0:T(8,128)S(1)}, f32[12,768]{1,0:T(8,128)}, u32[]{:S(2)}) copy-start(f32[12,768]{1,0:T(8,128)} %vec_ref.5) | copy-start | bytes 110596
  383.4 17.3 %copy-start.1 = (f32[12,384]{1,0:T(8,128)S(1)}, f32[12,384]{1,0:T(8,128)}, u32[]{:S(2)}) copy-start(f32[12,384]{1,0:T(8,128)} %param.18) | copy-start | bytes 55300
  383.4 17.3 %copy-start.2 = (f32[12,384]{1,0:T(8,128)S(1)}, f32[12,384]{1,0:T(8,128)}, u32[]{:S(2)}) copy-start(f32[12,384]{1,0:T(8,128)} %param.19) | copy-start | bytes 55300
  383.5 17.3 %copy-start.3 = (f32[16,768]{1,0:T(8,128)S(1)}, f32[16,768]{1,0:T(8,128)}, u32[]{:S(2)}) copy-start(f32[16,768]{1,0:T(8,128)} %get-tuple-element.61) | copy-start | bytes 147460

commit v2 on v0

--- a/solution.py
+++ b/solution.py
@@ -649,6 +649,7 @@
 FRONT_PAIRS = (2, 4, 5, 6, 7, 8)
 FRONT_REST = (6, 7, 8, 9, 10, 11, 12, 13, 14)
 FRONT_LEAD = 9
+FRONT_PHASES = 4
 
 
 def front_kernel(
@@ -723,19 +724,20 @@
         sems = (two_send.at[group], two_recv.at[group])
         return Item(place, two.at[span_of], two_kept.at[span_of], two_land.at[:, span_of], sems, load, store)
 
-    def tick(number, odd):
+    def tick(number, phase):
         for chunk in range(CHUNKS):
-            if odd == 0 and 0 <= number - 2 * chunk <= 2:
+            if phase == 0 and 0 <= number - 2 * chunk <= 2:
                 spread.step(chunk, number - 2 * chunk)
-        starts = [(pair_item, group, start) for group, start in enumerate(FRONT_PAIRS)]
-        starts += [(rest_item, group, start) for group, start in enumerate(FRONT_REST)]
-        for make, group, start in starts:
-            if group % 2 == odd and 0 <= number - start < Item.steps:
-                make(group).step(number - start)
+        for index, start in enumerate(FRONT_PAIRS):
+            if index % 2 * 2 == phase and 0 <= number - start < Item.steps:
+                pair_item(index).step(number - start)
+        for index, start in enumerate(FRONT_REST):
+            if (index + 1) % FRONT_PHASES == phase and 0 <= number - start < Item.steps:
+                rest_item(index).step(number - start)
 
     def both(number):
-        tick(number, 0)
-        tick(number, 1)
+        for phase in range(FRONT_PHASES):
+            tick(number, phase)
 
     @pl.when(grid_step == 0)
     def lead():
@@ -833,9 +835,9 @@
         peak = score_block(0, block, peak)
     before = None
     for unit, (head, step) in enumerate(units):
-        if unit == 2:
+        if unit > 0:
             for number in range(2 * PAIRS):
-                pl.when(grid_step == number)(partial(tick, FRONT_LEAD + number, 1))
+                pl.when(grid_step == number)(partial(tick, FRONT_LEAD + number, unit))
         here = slice(step * half, (step + 1) * half)
         top = jnp.max(peak, 0, keepdims=True)
         total = jnp.zeros((8, half), f32)
@@ -1099,7 +1101,7 @@
 BACK_TAIL = 4
 BACK_PAIRS = tuple((index, 1) for index in range(PAIRS))
 BACK_REST = (0, 1, 2, 3, 4, 5, 6, 7, 8)
-BACK_HAND = 15
+BACK_HANDS = (14, 17, 20)
 
 
 def back_kernel(
@@ -1207,8 +1209,8 @@
                 for index in range(first, first + count):
                     for tile in range(3):
                         pair_store(index, tile).start()
-        if odd == 0 and 0 <= number - BACK_HAND < Hand.steps:
-            hand.step(number - BACK_HAND)
+        if odd == 0 and number in BACK_HANDS:
+            hand.step(BACK_HANDS.index(number))
         for group, start in enumerate(BACK_REST):
             if odd == 1 and number == max(start - 1, 0):
                 load_two(group).start()

time: 401 us -> 395 us (0.985)
  Pallas kernels: 396 us -> 390 us
where the time goes in v2:
time: 395 us; the launch traced here: 394 us
  Pallas kernels  390 us (99%)
    pallas_call x1, Pallas kernels, back(): pl.pallas_call(back_kernel, grid=(BACK_STEPS + BACK_TAIL,), in_specs=[sme...  151 us
    pallas_call x1, Pallas kernels, front(): pl.pallas_call(front_kernel, grid=(PAIRS, rows), in_specs=[smem, smem, pl...  126 us
    pallas_call x1, Pallas kernels, feed(): pl.pallas_call(feed_kernel, grid=(tokens // size,), in_specs=[token_block...  96 us
    pallas_call x1, Pallas kernels, update(): pl.pallas_call(update_kernel, grid_spec=pltpu.PrefetchScalarGridSpec(num_...  17.3 us

profile of v2, /device:TPU:0, one launch (start us, length us, event | category | flops | bytes accessed | tf_op | source)
XLA Modules:
  0.0 394.4 jit_solution(4282303809227478363)
XLA Ops:
  0.6 1.3 copy.19.lengths
  2.0 126.2 %front.1 = (bf16[2,1024,768]{2,1,0:T(8,128)(2,1)}, bf16[2,1024,768]{2,1,0:T(8,128)(2,1)}, bf16[2048,768]{1,0:T(8,128)(2,1)}, bf16[6,768,384]{2,1,0:T(8,128)(2,1)...) custom-call(s32[12]{0:T(128)} %owner.1, ...), custom_call_target="tpu_custom_call" | custom-call | tf_op jit(solution)/shard_map/front/pallas_call | solution.py:884
  128.2 0.0 copy-start.4
  128.2 96.0 %feed.1 = (bf16[2048,768]{1,0:T(8,128)(2,1)}, bf16[2048,768]{1,0:T(8,128)(2,1)}, bf16[768,2048]{1,0:T(8,128)(2,1)}, f32[16,768]{1,0:T(8,128)}, bf16[9,768,768]{2,1,0:T(8,128)(2,1)}) custom-call(bf16[2048,768]{1,0:T(8,128)(2,1)} %get-tuple-element.41.c_ref, bf16[768,2048]{1,0:T(8,128)(2,1)} %get-tuple-element.40.o_ref, bf16[2048,768]{1,0:T(8,128)(2,1)} %bitcast.7, ...), custom_call_target="tpu_custom_call" | custom-call | flops 65229815808 | bytes 49545216 | tf_op jit(solution)/shard_map/feed/pallas_call | solution.py:402
  224.2 0.0 copy-done.4
  224.2 0.2 convert_reduce_fusion
  224.4 0.1 select_reduce_fusion
  224.5 0.5 add_maximum_fusion
  225.0 150.6 %back.1 = (bf16[4,512,768]{2,1,0:T(8,128)(2,1)}, bf16[4,512,768]{2,1,0:T(8,128)(2,1)}, bf16[3,384,768]{2,1,0:T(8,128)(2,1)}, bf16[3,384,768]{2,1,0:T(8,128)(2,1)}, f32[16,768]{1,0:T(8,128)}) custom-call(s32[48]{0:T(128)} %get-tuple-element.65.table, bf16[24,1024,1024]{2,1,0:T(8,128)(2,1)} %get-tuple-element.35.p_ref, ...), custom_call_target="tpu_custom_call" | custom-call | tf_op jit(solution)/shard_map/back/pallas_call | solution.py:1450
  375.7 0.6 dynamic_slice.9.tile_at
  376.3 0.0 copy-start
  376.3 0.0 copy-start.1
  376.3 0.0 copy-start.2
  376.3 0.0 copy-start.3
  376.3 17.3 %update.1 = (f32[3,384,768]{2,1,0:T(8,128)}, f32[3,384,768]{2,1,0:T(8,128)}, f32[3,384,768]{2,1,0:T(8,128)}, f32[2048,768]{1,0:T(8,128)}, f32[2048,768]{1,0:T(8,128)}) custom-call(s32[3]{0:T(128)} %dynamic_slice.9.tile_at, bf16[3,384,768]{2,1,0:T(8,128)(2,1)} %get-tuple-element.52.one, bf16[3,384,768]{2,1,0:T(8,128)(2,1)} %get-tuple-element.53.two, ...), custom_call_target="tpu_custom_call" | custom-call | tf_op jit(solution)/shard_map/update/pallas_call | solution.py:1551
  393.5 0.0 copy-done
  393.5 0.0 copy-done.1
  393.6 0.0 copy-done.2
  393.6 0.0 copy-done.3
  393.6 0.6 multiply_subtract_fusion
  (1 shorter events, 0.0 us)
Async XLA Ops:
  128.2 96.1 %copy-start.4 = (s32[12]{0:T(128)S(1)}, s32[12]{0:T(128)}, u32[]{:S(2)}) copy-start(s32[12]{0:T(128)} %owner.1) | copy-start | bytes 148
  376.3 17.3 %copy-start = (f32[12,768]{1,0:T(8,128)S(1)}, f32[12,768]{1,0:T(8,128)}, u32[]{:S(2)}) copy-start(f32[12,768]{1,0:T(8,128)} %vec_ref.5) | copy-start | bytes 110596
  376.3 17.3 %copy-start.1 = (f32[12,384]{1,0:T(8,128)S(1)}, f32[12,384]{1,0:T(8,128)}, u32[]{:S(2)}) copy-start(f32[12,384]{1,0:T(8,128)} %param.18) | copy-start | bytes 55300
  376.3 17.3 %copy-start.2 = (f32[12,384]{1,0:T(8,128)S(1)}, f32[12,384]{1,0:T(8,128)}, u32[]{:S(2)}) copy-start(f32[12,384]{1,0:T(8,128)} %param.19) | copy-start | bytes 55300
  376.3 17.3 %copy-start.3 = (f32[16,768]{1,0:T(8,128)S(1)}, f32[16,768]{1,0:T(8,128)}, u32[]{:S(2)}) copy-start(f32[16,768]{1,0:T(8,128)} %get-tuple-element.61) | copy-start | bytes 147460

commit v3 on v2

--- a/solution.py
+++ b/solution.py
@@ -649,6 +649,7 @@
 FRONT_PAIRS = (2, 4, 5, 6, 7, 8)
 FRONT_REST = (6, 7, 8, 9, 10, 11, 12, 13, 14)
 FRONT_LEAD = 9
+FRONT_CHUNKS = ((0, 1, 2), (1, 3, 4), (3, 5, 6))
 FRONT_PHASES = 4
 
 
@@ -725,9 +726,9 @@
         return Item(place, two.at[span_of], two_kept.at[span_of], two_land.at[:, span_of], sems, load, store)
 
     def tick(number, phase):
-        for chunk in range(CHUNKS):
-            if phase == 0 and 0 <= number - 2 * chunk <= 2:
-                spread.step(chunk, number - 2 * chunk)
+        for chunk, ticks in enumerate(FRONT_CHUNKS):
+            if phase == 0 and number in ticks:
+                spread.step(chunk, ticks.index(number))
         for index, start in enumerate(FRONT_PAIRS):
             if index % 2 * 2 == phase and 0 <= number - start < Item.steps:
                 pair_item(index).step(number - start)

time: 395 us -> 392 us (level)
  no operation moved by 1% of the time
where the time goes in v3:
time: 392 us; the launch traced here: 391 us
  Pallas kernels  387 us (99%)
    pallas_call x1, Pallas kernels, back(): pl.pallas_call(back_kernel, grid=(BACK_STEPS + BACK_TAIL,), in_specs=[sme...  150 us
    pallas_call x1, Pallas kernels, front(): pl.pallas_call(front_kernel, grid=(PAIRS, rows), in_specs=[smem, smem, pl...  123 us
    pallas_call x1, Pallas kernels, feed(): pl.pallas_call(feed_kernel, grid=(tokens // size,), in_specs=[token_block...  96 us
    pallas_call x1, Pallas kernels, update(): pl.pallas_call(update_kernel, grid_spec=pltpu.PrefetchScalarGridSpec(num_...  17.3 us

profile of v3, /device:TPU:0, one launch (start us, length us, event | category | flops | bytes accessed | tf_op | source)
XLA Modules:
  0.0 391.2 jit_solution(15708695018453299261)
XLA Ops:
  0.6 1.3 copy.19.lengths
  2.0 123.2 %front.1 = (bf16[2,1024,768]{2,1,0:T(8,128)(2,1)}, bf16[2,1024,768]{2,1,0:T(8,128)(2,1)}, bf16[2048,768]{1,0:T(8,128)(2,1)}, bf16[6,768,384]{2,1,0:T(8,128)(2,1)...) custom-call(s32[12]{0:T(128)} %owner.1, ...), custom_call_target="tpu_custom_call" | custom-call | tf_op jit(solution)/shard_map/front/pallas_call | solution.py:885
  125.2 0.0 copy-start.4
  125.2 96.0 %feed.1 = (bf16[2048,768]{1,0:T(8,128)(2,1)}, bf16[2048,768]{1,0:T(8,128)(2,1)}, bf16[768,2048]{1,0:T(8,128)(2,1)}, f32[16,768]{1,0:T(8,128)}, bf16[9,768,768]{2,1,0:T(8,128)(2,1)}) custom-call(bf16[2048,768]{1,0:T(8,128)(2,1)} %get-tuple-element.41.c_ref, bf16[768,2048]{1,0:T(8,128)(2,1)} %get-tuple-element.40.o_ref, bf16[2048,768]{1,0:T(8,128)(2,1)} %bitcast.7, ...), custom_call_target="tpu_custom_call" | custom-call | flops 65229815808 | bytes 49545216 | tf_op jit(solution)/shard_map/feed/pallas_call | solution.py:402
  221.2 0.0 copy-done.4
  221.2 0.2 convert_reduce_fusion
  221.4 0.1 select_reduce_fusion
  221.5 0.5 add_maximum_fusion
  222.0 150.4 %back.1 = (bf16[4,512,768]{2,1,0:T(8,128)(2,1)}, bf16[4,512,768]{2,1,0:T(8,128)(2,1)}, bf16[3,384,768]{2,1,0:T(8,128)(2,1)}, bf16[3,384,768]{2,1,0:T(8,128)(2,1)}, f32[16,768]{1,0:T(8,128)}) custom-call(s32[48]{0:T(128)} %get-tuple-element.65.table, bf16[24,1024,1024]{2,1,0:T(8,128)(2,1)} %get-tuple-element.35.p_ref, ...), custom_call_target="tpu_custom_call" | custom-call | tf_op jit(solution)/shard_map/back/pallas_call | solution.py:1451
  372.4 0.6 dynamic_slice.9.tile_at
  373.0 0.0 copy-start
  373.0 0.0 copy-start.1
  373.0 0.0 copy-start.2
  373.0 0.0 copy-start.3
  373.0 17.3 %update.1 = (f32[3,384,768]{2,1,0:T(8,128)}, f32[3,384,768]{2,1,0:T(8,128)}, f32[3,384,768]{2,1,0:T(8,128)}, f32[2048,768]{1,0:T(8,128)}, f32[2048,768]{1,0:T(8,128)}) custom-call(s32[3]{0:T(128)} %dynamic_slice.9.tile_at, bf16[3,384,768]{2,1,0:T(8,128)(2,1)} %get-tuple-element.52.one, bf16[3,384,768]{2,1,0:T(8,128)(2,1)} %get-tuple-element.53.two, ...), custom_call_target="tpu_custom_call" | custom-call | tf_op jit(solution)/shard_map/update/pallas_call | solution.py:1552
  390.3 0.0 copy-done
  390.3 0.0 copy-done.1
  390.3 0.0 copy-done.2
  390.3 0.0 copy-done.3
  390.3 0.6 multiply_subtract_fusion
  (1 shorter events, 0.0 us)
Async XLA Ops:
  125.2 96.1 %copy-start.4 = (s32[12]{0:T(128)S(1)}, s32[12]{0:T(128)}, u32[]{:S(2)}) copy-start(s32[12]{0:T(128)} %owner.1) | copy-start | bytes 148
  373.0 17.3 %copy-start = (f32[12,768]{1,0:T(8,128)S(1)}, f32[12,768]{1,0:T(8,128)}, u32[]{:S(2)}) copy-start(f32[12,768]{1,0:T(8,128)} %vec_ref.5) | copy-start | bytes 110596
  373.0 17.3 %copy-start.1 = (f32[12,384]{1,0:T(8,128)S(1)}, f32[12,384]{1,0:T(8,128)}, u32[]{:S(2)}) copy-start(f32[12,384]{1,0:T(8,128)} %param.18) | copy-start | bytes 55300
  373.0 17.3 %copy-start.2 = (f32[12,384]{1,0:T(8,128)S(1)}, f32[12,384]{1,0:T(8,128)}, u32[]{:S(2)}) copy-start(f32[12,384]{1,0:T(8,128)} %param.19) | copy-start | bytes 55300
  373.0 17.3 %copy-start.3 = (f32[16,768]{1,0:T(8,128)S(1)}, f32[16,768]{1,0:T(8,128)}, u32[]{:S(2)}) copy-start(f32[16,768]{1,0:T(8,128)} %get-tuple-element.61) | copy-start | bytes 147460
